TPU v7x, 128 devices: a whole 4x4x4 slice. The times are simulated.
128 devices in a mesh: gx: 16 (over z, y), gy: 8 (over x, core).
Axes of the slice: x: 4, y: 4, z: 4, core: 2. Of those that a mesh axis runs over, the one named last changes fastest.
Arguments:
- velocity: float32 [2, 2048, 2048], P(None, 'gy', 'gx'), may hold values from -6 to 6
- residual: float32 [2, 2048, 2048], P(None, 'gy', 'gx'), may hold values from -6 to 6
- east_visc: float32 [2048, 2048], P('gy', 'gx'), may hold values from 0.5 to 4
- north_visc: float32 [2048, 2048], P('gy', 'gx'), may hold values from 0.5 to 4
- coriolis: float32 [2048, 2048], P('gy', 'gx'), may hold values from 0.2 to 0.6
- land: int32 [2048, 2048], P('gy', 'gx'), may hold values 0 or 1
- ocean_velocity: float32 [2, 2048, 2048], P(None, ('gx', 'gy')), may hold values from -4 to 4
- ocean_owner: int32 [2048, 2048], P(('gx', 'gy')), may hold values from 0 to 15
- tile_drag: float32 [16], replicated, may hold values from 0.5 to 2
Outputs:
- velocity_out: float32 [2, 2048, 2048], P(None, 'gy', 'gx')
- ocean_stress: float32 [2, 2048, 2048], P(None, ('gx', 'gy'))
All inputs are finite; a program needn't handle non-finite values. No bound on the sum of `land` on one device may be relied on, other than what follows from the above.
Results may differ from a plain program's by a relative error of at most 0.00002.
Values sent between devices are 32-bit elements; how exact they have to be, the bound alone decides.
A program may use at most 192 MiB of HBM per device.

v0:
```python
import math

import jax
import jax.numpy as jnp
from jax import lax
from jax.sharding import PartitionSpec as P

LEVELS = 6
AGG_LEVEL = 3
OTILES = 16


mass_term = 0.001
relax = 0.7
cos_turn = math.cos(0.42)
sin_turn = math.sin(0.42)


def shifted(block, axis, distance):
    devices = range(lax.axis_size(axis))
    route = [(i - distance, i) for i in devices if i - distance in devices]
    return lax.ppermute(block, axis, route)


def padded_2(block, sides, width):
    for axis, dim in sides:
        count = lax.axis_size(axis)
        forward = [(i, i + 1) for i in range(count - 1)]
        backward = [(target, source) for source, target in forward]
        low = lax.ppermute(
            lax.slice_in_dim(block, block.shape[dim] - width, None, axis=dim), axis, forward
        )
        high = lax.ppermute(lax.slice_in_dim(block, 0, width, axis=dim), axis, backward)
        block = jnp.concatenate([low, block, high], axis=dim)
    return block


def coarsen(east, north, spin):
    rows, cols = east.shape
    east_four = east.reshape(rows // 2, 2, cols // 2, 2)
    north_four = north.reshape(rows // 2, 2, cols // 2, 2)
    east_next = (east_four[:, 0, :, 1] + east_four[:, 1, :, 1]) * 0.25
    north_next = (north_four[:, 1, :, 0] + north_four[:, 1, :, 1]) * 0.25
    spin_next = spin.reshape(rows // 2, 2, cols // 2, 2).mean(axis=(1, 3)) * 0.5
    return (east_next, north_next, spin_next)


def restrict(field):
    rows, cols = (field.shape[1], field.shape[2])
    return field.reshape(2, rows // 2, 2, cols // 2, 2).mean(axis=(2, 4))


def prolong(field):
    return jnp.repeat(jnp.repeat(field, 2, axis=1), 2, axis=2)


def block_step(res, diag, spin):
    det = diag * diag + spin * spin
    first = (diag * res[0] + spin * res[1]) / det
    second = (diag * res[1] - spin * res[0]) / det
    return relax * jnp.stack([first, second])


def apply_padded(field, padded, faces):
    east, west, north, south, spin, diag = faces
    out = diag * field - east * padded[:, 1:-1, 2:] - west * padded[:, 1:-1, :-2]
    out = out - north * padded[:, 2:, 1:-1] - south * padded[:, :-2, 1:-1]
    return out + jnp.stack([-spin * field[1], spin * field[0]])


def grid_faces(east, north, spin):
    west = jnp.pad(east, ((0, 0), (1, 0)))[:, :-1]
    south = jnp.pad(north, ((1, 0), (0, 0)))[:-1]
    diag = mass_term + east + west + north + south
    return (east, west, north, south, spin, diag)


def apply_grid(field, faces):
    padded = jnp.pad(field, ((0, 0), (1, 1), (1, 1)))
    return apply_padded(field, padded, faces)


def masked(value, ocean):
    if ocean is None:
        return value
    return value * ocean


def grid_cycle(rhs, east, north, spin, level):
    faces = grid_faces(east, north, spin)
    diag = faces[5]
    if level == LEVELS - 1:
        field = block_step(rhs, diag, spin)
        sweeps = max(8, east.shape[1] // 4)

        def sweep_once(index, state):
            return state + block_step(rhs - apply_grid(state, faces), diag, spin)

        return lax.fori_loop(0, sweeps - 1, sweep_once, field)
    field = block_step(rhs, diag, spin)
    field = field + block_step(rhs - apply_grid(field, faces), diag, spin)
    leftover = rhs - apply_grid(field, faces)
    east_next, north_next, spin_next = coarsen(east, north, spin)
    coarse = grid_cycle(restrict(leftover), east_next, north_next, spin_next, level + 1)
    field = field + prolong(coarse)
    for sweep in range(2):
        field = field + block_step(rhs - apply_grid(field, faces), diag, spin)
    return field


def tile_faces(east, north, spin):
    west_rim = shifted(east[:, -1:], "gx", 1)
    south_rim = shifted(north[-1:, :], "gy", 1)
    west = jnp.concatenate([west_rim, east[:, :-1]], axis=1)
    south = jnp.concatenate([south_rim, north[:-1, :]], axis=0)
    diag = mass_term + east + west + north + south
    return (east, west, north, south, spin, diag)


def apply_tile(field, faces):
    padded = padded_2(field, (("gy", 1), ("gx", 2)), 1)
    return apply_padded(field, padded, faces)


def collected(rhs, east, north, spin, level):
    rows, cols = east.shape
    along = (
        lax.all_gather(rhs, "gx", axis=2, tiled=True),
        lax.all_gather(east, "gx", axis=1, tiled=True),
        lax.all_gather(north, "gx", axis=1, tiled=True),
        lax.all_gather(spin, "gx", axis=1, tiled=True),
    )
    whole = (
        lax.all_gather(along[0], "gy", axis=1, tiled=True),
        lax.all_gather(along[1], "gy", axis=0, tiled=True),
        lax.all_gather(along[2], "gy", axis=0, tiled=True),
        lax.all_gather(along[3], "gy", axis=0, tiled=True),
    )
    whole_rhs, whole_east, whole_north, whole_spin = whole
    solved = grid_cycle(whole_rhs, whole_east, whole_north, whole_spin, level)
    row_start = lax.axis_index("gy") * rows
    col_start = lax.axis_index("gx") * cols
    return lax.dynamic_slice(solved, (jnp.int32(0), row_start, col_start), (2, rows, cols))


def tile_cycle(rhs, east, north, spin, level, stop, ocean):
    if level == stop:
        return collected(rhs, east, north, spin, level)
    faces = tile_faces(east, north, spin)
    diag = faces[5]
    field = masked(block_step(rhs, diag, spin), ocean)
    field = field + masked(block_step(rhs - apply_tile(field, faces), diag, spin), ocean)
    leftover = masked(rhs - apply_tile(field, faces), ocean)
    east_next, north_next, spin_next = coarsen(east, north, spin)
    coarse = tile_cycle(restrict(leftover), east_next, north_next, spin_next, level + 1, stop, None)
    field = field + masked(prolong(coarse), ocean)
    for sweep in range(2):
        field = field + masked(block_step(rhs - apply_tile(field, faces), diag, spin), ocean)
    return field


def on_device(
    velocity,
    residual,
    east_visc,
    north_visc,
    coriolis,
    land,
    ocean_velocity,
    ocean_owner,
    tile_drag,
):
    ocean = (1 - land).astype(jnp.float32)
    stop = AGG_LEVEL
    correction = tile_cycle(residual, east_visc, north_visc, coriolis, 0, stop, ocean)
    velocity_out = velocity + correction
    turned = jnp.transpose(velocity_out, (0, 2, 1))
    ice_cols = lax.all_to_all(turned, "gy", split_axis=1, concat_axis=2, tiled=True)
    drag = jnp.zeros(ocean_owner.shape, jnp.float32)
    for tile in range(OTILES):
        drag = drag + jnp.where(ocean_owner == tile, tile_drag[tile], jnp.float32(0.0))
    diff = ice_cols - ocean_velocity
    speed = jnp.sqrt(diff[0] * diff[0] + diff[1] * diff[1])
    scale = drag * speed
    ocean_stress = jnp.stack(
        [
            scale * (cos_turn * diff[0] - sin_turn * diff[1]),
            scale * (sin_turn * diff[0] + cos_turn * diff[1]),
        ]
    )
    return (velocity_out, ocean_stress)


def solution(mesh):
    placed = (
        P(None, "gy", "gx"),
        P(None, "gy", "gx"),
        P("gy", "gx"),
        P("gy", "gx"),
        P("gy", "gx"),
        P("gy", "gx"),
        P(None, ("gx", "gy"), None),
        P(("gx", "gy"), None),
        P(),
    )
    return jax.shard_map(
        on_device,
        mesh=mesh,
        in_specs=placed,
        out_specs=(P(None, "gy", "gx"), P(None, ("gx", "gy"), None)),
        check_vma=False,
    )
```

profile of v0, /device:TPU:32, one launch (start us, length us, event | category | flops | bytes accessed | tf_op | source)
XLA Modules:
  0.0 819.8 jit_solution(6874887858403188705)
XLA Ops:
  9.1 10.5 %reshape.806 = f32[128,2,64,2]{3,2,1,0:T(8,128)} reshape(f32[256,128]{1,0:T(8,128)} %param.13) | data formatting | bytes 262144 | tf_op jit(solution)/shard_map/reshape | solution.py:40
  19.6 9.0 %fusion.330 = (f32[128,1,64,1]{3,2,1,0:T(8,128)}, f32[128,1,64,1]{3,2,1,0:T(8,128)}) fusion(f32[128,2,64,2]{3,2,1,0:T(8,128)} %reshape.806), kind=kLoop, calls=%fused_computation.687 | loop fusion | bytes 131072 | tf_op jit(solution)/shard_map/slice | solution.py:42
  28.6 3.8 copy.731
  32.4 3.7 copy.732
  41.0 9.8 %reshape.807 = f32[128,2,64,2]{3,2,1,0:T(8,128)} reshape(f32[256,128]{1,0:T(8,128)S(1)} %copy-done.3) | data formatting | bytes 262144 | tf_op jit(solution)/shard_map/reshape | solution.py:41
  50.8 8.1 fusion.331
  58.9 3.7 copy.733
  62.6 3.8 copy.734
  67.1 3.9 collective-permute-start.7
  86.0 23.9 %all-gather.2 = f32[32,1,256,1]{0,3,1,2:T(1,128)S(1)} all-gather(f32[32,1,16,1]{0,3,1,2:T(1,128)S(1)} %bitcast.677), channel_id=4, replica_groups=mesh['gx'=16,'gy'=8] {'gx'}, dimensions={2}, use_global_device_ids=true | all-gather | bytes 34816 | tf_op jit(solution)/shard_map/all_gather | solution.py:130
  110.0 12.8 %all-gather.3 = f32[256,1,256,1]{2,0,3,1:T(8,128)S(1)} all-gather(f32[32,1,256,1]{2,0,3,1:T(8,128)S(1)} %copy.714), channel_id=5, replica_groups=mesh['gx'=16,'gy'=8] {'gy'}, dimensions={0}, use_global_device_ids=true | all-gather | bytes 294912 | tf_op jit(solution)/shard_map/all_gather | solution.py:136
  123.3 22.2 %all-gather = f32[32,1,256,1]{0,3,1,2:T(1,128)S(1)} all-gather(f32[32,1,16,1]{0,3,1,2:T(1,128)S(1)} %bitcast.678), channel_id=2, replica_groups=mesh['gx'=16,'gy'=8] {'gx'}, dimensions={2}, use_global_device_ids=true | all-gather | bytes 34816 | tf_op jit(solution)/shard_map/all_gather | solution.py:129
  145.6 13.4 %all-gather.1 = f32[256,1,256,1]{2,0,3,1:T(8,128)S(1)} all-gather(f32[32,1,256,1]{2,0,3,1:T(8,128)S(1)} %copy.710), channel_id=3, replica_groups=mesh['gx'=16,'gy'=8] {'gy'}, dimensions={0}, use_global_device_ids=true | all-gather | bytes 294912 | tf_op jit(solution)/shard_map/all_gather | solution.py:135
  158.9 18.1 %reshape.813 = f32[128,2,128,2]{3,2,1,0:T(8,128)} reshape(f32[256,1,256,1]{2,0,3,1:T(8,128)S(1)} %all-gather.3) | data formatting | bytes 524288 | tf_op jit(solution)/shard_map/reshape | solution.py:41
  177.0 8.1 fusion.16
  185.2 18.1 %reshape.812 = f32[128,2,128,2]{3,2,1,0:T(8,128)} reshape(f32[256,1,256,1]{2,0,3,1:T(8,128)S(1)} %all-gather.1) | data formatting | bytes 524288 | tf_op jit(solution)/shard_map/reshape | solution.py:40
  203.3 10.2 %fusion.18 = f32[128,128]{1,0:T(8,128)S(1)} fusion(f32[128,2,128,2]{3,2,1,0:T(8,128)} %reshape.812), kind=kLoop, calls=%fused_computation.31 | loop fusion | flops 32768 | bytes 196608 | tf_op jit(solution)/shard_map/mul | solution.py:42
  213.5 5.5 mul.2038
  219.8 5.5 mul.2035
  225.3 9.9 %reshape.809 = f32[128,2,64,2]{3,2,1,0:T(8,128)} reshape(f32[256,128]{1,0:T(8,128)S(1)} %copy-done) | data formatting | bytes 262144 | tf_op jit(solution)/shard_map/reshape | solution.py:44
  235.2 4.5 reduce_sum.91
  248.4 6.9 fusion.20
  255.3 22.2 %all_gather.30 = f32[32,256]{0,1:T(8,128)S(1)} all-gather(f32[32,16]{0,1:T(8,128)S(1)} %broadcast_multiply_fusion.14), channel_id=1, replica_groups=mesh['gx'=16,'gy'=8] {'gx'}, dimensions={1}, use_global_device_ids=true | all-gather | bytes 34816 | tf_op jit(solution)/shard_map/all_gather | solution.py:131
  281.4 14.6 %all_gather.31 = f32[256,256]{1,0:T(8,128)S(1)} all-gather(f32[32,256]{1,0:T(8,128)S(1)} %copy.717), channel_id=1, replica_groups=mesh['gx'=16,'gy'=8] {'gy'}, dimensions={0}, use_global_device_ids=true | all-gather | bytes 294912 | tf_op jit(solution)/shard_map/all_gather | solution.py:137
  303.6 4.7 collective-permute-done.4
  308.3 5.2 collective-permute-done.5
  323.3 3.9 collective-permute-start.11
  327.3 3.9 collective-permute-done.10
  336.5 18.3 %reshape.808 = f32[2,128,2,64,2]{4,3,2,1,0:T(8,128)} reshape(f32[2,256,128]{2,1,0:T(8,128)S(1)} %fusion.109) | data formatting | bytes 524288 | tf_op jit(solution)/shard_map/reshape | solution.py:50
  354.8 8.1 reduce_sum.90
  379.0 5.0 collective-permute-done.15
  394.2 3.9 collective-permute-start.21
  399.3 4.0 collective-permute-done.21
  403.7 5.6 reshape.810
  423.0 3.9 collective-permute-start.25
  435.6 18.1 %reshape.815 = f32[128,2,128,2]{3,2,1,0:T(8,128)} reshape(f32[256,256]{1,0:T(8,128)S(1)} %all_gather.31) | data formatting | bytes 524288 | tf_op jit(solution)/shard_map/reshape | solution.py:44
  453.7 8.0 reduce_sum.97
  463.8 3.9 collective-permute-start.29
  467.7 3.7 collective-permute-done.29
  475.1 22.3 %all_gather.28 = f32[2,32,256]{1,0,2:T(2,128)S(1)} all-gather(f32[2,32,16]{1,0,2:T(2,128)S(1)} %copy.715), channel_id=1, replica_groups=mesh['gx'=16,'gy'=8] {'gx'}, dimensions={2}, use_global_device_ids=true | all-gather | bytes 69632 | tf_op jit(solution)/shard_map/all_gather | solution.py:128
  497.5 14.5 %all_gather.29 = f32[2,256,256]{2,1,0:T(8,128)S(1)} all-gather(f32[2,32,256]{2,1,0:T(8,128)S(1)} %copy.716), channel_id=1, replica_groups=mesh['gx'=16,'gy'=8] {'gy'}, dimensions={1}, use_global_device_ids=true | all-gather | bytes 589824 | tf_op jit(solution)/shard_map/all_gather | solution.py:134
  515.8 35.6 %reshape.814 = f32[2,128,2,128,2]{4,3,2,1,0:T(8,128)} reshape(f32[2,256,256]{2,1,0:T(8,128)} %fusion.41) | data formatting | bytes 1048576 | tf_op jit(solution)/shard_map/reshape | solution.py:50
  551.4 13.9 %reduce_sum.96 = f32[2,128,128]{2,1,0:T(8,128)} reduce(f32[2,128,2,128,2]{4,3,2,1,0:T(8,128)} %reshape.814, f32[]{:T(128)} %constant.42.clone.1), dimensions={2,4}, to_apply=%region_6.7 | reduce | flops 98304 | bytes 655364 | tf_op jit(solution)/shard_map/reduce_sum | solution.py:50
  572.4 10.5 %reshape.816 = f32[2,64,2,64,2]{4,3,2,1,0:T(8,128)} reshape(f32[2,128,128]{2,1,0:T(8,128)} %fusion.146) | data formatting | bytes 262144 | tf_op jit(solution)/shard_map/reshape | solution.py:50
  582.9 4.5 reduce_sum.98
  588.1 6.3 mul.2050
  600.9 39.7 %while.13 = (s32[]{:T(128)}, f32[2,64,64]{2,1,0:T(8,128)S(1)}, f32[64,64]{1,0:T(8,128)}, f32[64,64]{1,0:T(8,128)}, f32[64,64]{1,0:T(8,128)}, /*index=5*/f32[64,6...) while((s32[]{:T(128)}, f32[2,64,64]{2,1,0:T(8,128)S(1)}, ...), condition=%wide.region_11.12_spmd, body=%wide.region_10.11_spmd.sunk | while | flops 163842 | bytes 524405 | solution.py:99
  669.3 4.0 collective-permute-start.32
  675.3 5.6 collective-permute-done.33
  692.0 3.9 collective-permute-start.37
  711.9 3.9 collective-permute-start.41
  717.0 4.0 collective-permute-done.41
  731.3 3.9 collective-permute-start.45
  736.4 4.0 collective-permute-done.45
  750.3 3.9 collective-permute-start.49
  754.2 3.9 collective-permute-done.48
  758.2 4.0 collective-permute-done.49
  771.8 3.9 collective-permute-start.53
  775.8 3.9 collective-permute-done.52
  779.7 4.0 collective-permute-done.53
  785.1 4.6 all-to-all-start
  790.4 6.8 all-to-all-done
  798.3 10.3 %fusion.233 = f32[1,16,2048]{2,1,0:T(8,128)S(1)} fusion(f32[2,16,2048]{2,1,0:T(8,128)S(1)} %sub.552, f32[]{:T(128)} %bitcast.133, s32[16,2048]{1,0:T(8,128)S(1)} %copy-done.58, f32[]{:T(128)} %bitcast.132, f32[]{:T(128)} %bitcast.131, f32[]{:T(128)} %bitcast.130, f32[]{:T(128)} %bitcast.129, f32[]{:T(128)} %bitcast.128, f32[]{:T(128)} %bitcast.127, ...), kind=kLoop, calls=%fused_computation.421 | loop fusion | flops 1802240 | bytes 524352 | tf_op jit(solution)/shard_map/stack | solution.py:185
  808.6 10.3 %fusion.232 = f32[1,16,2048]{2,1,0:T(8,128)S(1)} fusion(f32[2,16,2048]{2,1,0:T(8,128)S(1)} %sub.552, f32[]{:T(128)} %bitcast.133, s32[16,2048]{1,0:T(8,128)S(1)} %copy-done.58, f32[]{:T(128)} %bitcast.132, f32[]{:T(128)} %bitcast.131, f32[]{:T(128)} %bitcast.130, f32[]{:T(128)} %bitcast.129, f32[]{:T(128)} %bitcast.128, f32[]{:T(128)} %bitcast.127, ...), kind=kLoop, calls=%fused_computation.419 | loop fusion | flops 1802240 | bytes 524352 | tf_op jit(solution)/shard_map/stack | solution.py:185
  (512 shorter events, 270.4 us)
Async XLA Ops:
  2.3 275.3 %collective-permute-start = (f32[256,1]{1,0:T(8,128)}, f32[256,1]{1,0:T(8,128)}, u32[]{:S(2)}, u32[]{:S(2)}) collective-permute-start(f32[256,1]{1,0:T(8,128)} %slice.964), channel_id=1, source_target_pairs={{0,8},{8,16},{16,24},{24,32},{32,40},{40,48},{48,56},{56,64},{64,7... | collective-permute-start | bytes 3080 | tf_op jit(solution)/shard_map/ppermute | solution.py:22
  7.0 270.5 %collective-permute-start.1 = (f32[1,128]{1,0:T(1,128)}, f32[1,128]{1,0:T(1,128)}, u32[]{:S(2)}, u32[]{:S(2)}) collective-permute-start(f32[1,128]{1,0:T(1,128)} %slice.966), channel_id=1, source_target_pairs={{0,1},{1,2},{2,3},{3,4},{4,5},{5,6},{6,7},{8,9},{9,10},{10,11},{11... | collective-permute-start | bytes 1544 | tf_op jit(solution)/shard_map/ppermute | solution.py:22
  36.8 366.5 %copy-start.11 = (f32[128,64]{1,0:T(8,128)}, f32[128,64]{1,0:T(8,128)S(1)}, u32[]{:S(2)}) copy-start(f32[128,64]{1,0:T(8,128)S(1)} %copy.690) | copy-start | bytes 98308
  37.5 325.4 %collective-permute-start.6 = (f32[128,1]{1,0:T(8,128)}, f32[128,1]{1,0:T(8,128)}, u32[]{:S(2)}, u32[]{:S(2)}) collective-permute-start(f32[128,1]{1,0:T(8,128)} %slice.1246), channel_id=1, source_target_pairs={{0,8},{8,16},{16,24},{24,32},{32,40},{40,48},{48,56},{56,64},{64,7... | collective-permute-start | bytes 1544 | tf_op jit(solution)/shard_map/ppermute | solution.py:22
  67.1 295.8 %collective-permute-start.7 = (f32[1,64]{1,0:T(1,128)}, f32[1,64]{1,0:T(1,128)}, u32[]{:S(2)}, u32[]{:S(2)}) collective-permute-start(f32[1,64]{1,0:T(1,128)} %bitcast.143), channel_id=1, source_target_pairs={{0,1},{1,2},{2,3},{3,4},{4,5},{5,6},{6,7},{8,9},{9,10},{10,11},{11... | collective-permute-start | bytes 776 | tf_op jit(solution)/shard_map/ppermute | solution.py:22
  74.9 337.3 %collective-permute-start.16 = (f32[64,1]{0,1:T(1,128)}, f32[64,1]{0,1:T(1,128)}, u32[]{:S(2)}, u32[]{:S(2)}) collective-permute-start(f32[64,1]{0,1:T(1,128)} %slice.1270), channel_id=1, source_target_pairs={{0,8},{8,16},{16,24},{24,32},{32,40},{40,48},{48,56},{56,64},{64,7... | collective-permute-start | bytes 776 | tf_op jit(solution)/shard_map/ppermute | solution.py:22
  78.1 235.9 %copy-start.8 = (f32[256,128]{1,0:T(8,128)}, f32[256,128]{1,0:T(8,128)S(1)}, u32[]{:S(2)}) copy-start(f32[256,128]{1,0:T(8,128)S(1)} %broadcast_multiply_fusion.3) | copy-start | bytes 393220
  84.9 92.1 %copy-start.48 = (f32[64,32]{0,1:T(8,128)}, f32[64,32]{0,1:T(8,128)S(1)}, u32[]{:S(2)}) copy-start(f32[64,32]{0,1:T(8,128)S(1)} %get-tuple-element.218) | copy-start | bytes 24580
  278.8 18.7 %collective-permute-start.2 = (f32[2,1,128]{2,1,0:T(1,128)S(1)}, f32[2,1,128]{2,1,0:T(1,128)S(1)}, u32[]{:S(2)}, u32[]{:S(2)}) collective-permute-start(f32[2,1,128]{2,1,0:T(1,128)S(1)} %get-tuple-element.305), channel_id=1, source_target_pairs={{0,1},{1,2},{2,3},{3,4},{4,5},{5,6},{6,7},{8,9},{9,10},{10,11},{11... | collective-permute-start | bytes 3080 | tf_op jit(solution)/shard_map/ppermute | solution.py:30
  280.1 17.4 %collective-permute-start.3 = (f32[2,1,128]{2,1,0:T(1,128)S(1)}, f32[2,1,128]{2,1,0:T(1,128)S(1)}, u32[]{:S(2)}, u32[]{:S(2)}) collective-permute-start(f32[2,1,128]{2,1,0:T(1,128)S(1)} %get-tuple-element.304), channel_id=1, source_target_pairs={{1,0},{2,1},{3,2},{4,3},{5,4},{6,5},{7,6},{9,8},{10,9},{11,10},{12... | collective-permute-start | bytes 3080 | tf_op jit(solution)/shard_map/ppermute | solution.py:33
  297.7 10.6 %collective-permute-start.4 = (f32[2,258,1]{2,1,0:T(8,128)S(1)}, f32[2,258,1]{2,1,0:T(8,128)S(1)}, u32[]{:S(2)}, u32[]{:S(2)}) collective-permute-start(f32[2,258,1]{2,1,0:T(8,128)S(1)} %get-tuple-element.280), channel_id=1, source_target_pairs={{8,0},{16,8},{24,16},{32,24},{40,32},{48,40},{56,48},{64,56},{72,6... | collective-permute-start | bytes 6200 | tf_op jit(solution)/shard_map/ppermute | solution.py:33
  301.1 12.5 %collective-permute-start.5 = (f32[2,258,1]{2,1,0:T(8,128)S(1)}, f32[2,258,1]{2,1,0:T(8,128)S(1)}, u32[]{:S(2)}, u32[]{:S(2)}) collective-permute-start(f32[2,258,1]{2,1,0:T(8,128)S(1)} %get-tuple-element.281), channel_id=1, source_target_pairs={{0,8},{8,16},{16,24},{24,32},{32,40},{40,48},{48,56},{56,64},{64,7... | collective-permute-start | bytes 6200 | tf_op jit(solution)/shard_map/ppermute | solution.py:30
  314.1 7.1 collective-permute-start.8
  315.4 5.8 collective-permute-start.9
  319.7 83.6 %copy-start.19 = (f32[128,64]{1,0:T(8,128)}, f32[128,64]{1,0:T(8,128)S(1)}, u32[]{:S(2)}) copy-start(f32[128,64]{1,0:T(8,128)S(1)} %copy.699) | copy-start | bytes 98308
  321.4 9.8 %collective-permute-start.10 = (f32[2,258,1]{2,1,0:T(8,128)S(1)}, f32[2,258,1]{2,1,0:T(8,128)S(1)}, u32[]{:S(2)}, u32[]{:S(2)}) collective-permute-start(f32[2,258,1]{2,1,0:T(8,128)S(1)} %get-tuple-element.278), channel_id=1, source_target_pairs={{8,0},{16,8},{24,16},{32,24},{40,32},{48,40},{56,48},{64,56},{72,6... | collective-permute-start | bytes 6200 | tf_op jit(solution)/shard_map/ppermute | solution.py:33
  323.3 11.9 %collective-permute-start.11 = (f32[2,258,1]{2,1,0:T(8,128)S(1)}, f32[2,258,1]{2,1,0:T(8,128)S(1)}, u32[]{:S(2)}, u32[]{:S(2)}) collective-permute-start(f32[2,258,1]{2,1,0:T(8,128)S(1)} %get-tuple-element.279), channel_id=1, source_target_pairs={{0,8},{8,16},{16,24},{24,32},{32,40},{40,48},{48,56},{56,64},{64,7... | collective-permute-start | bytes 6200 | tf_op jit(solution)/shard_map/ppermute | solution.py:30
  331.2 80.9 %collective-permute-start.17 = (f32[1,32]{0,1:T(8,128)}, f32[1,32]{0,1:T(8,128)S(1)}, u32[]{:S(2)}, u32[]{:S(2)}) collective-permute-start(f32[1,32]{0,1:T(8,128)} %bitcast.679), channel_id=1, source_target_pairs={{0,1},{1,2},{2,3},{3,4},{4,5},{5,6},{6,7},{8,9},{9,10},{10,11},{11... | collective-permute-start | bytes 392 | tf_op jit(solution)/shard_map/ppermute | solution.py:22
  364.0 5.5 collective-permute-start.12
  367.2 4.6 collective-permute-start.13
  372.0 7.0 collective-permute-start.14
  374.7 9.3 %collective-permute-start.15 = (f32[2,130,1]{2,1,0:T(8,128)S(1)}, f32[2,130,1]{2,1,0:T(8,128)S(1)}, u32[]{:S(2)}, u32[]{:S(2)}) collective-permute-start(f32[2,130,1]{2,1,0:T(8,128)S(1)} %get-tuple-element.329), channel_id=1, source_target_pairs={{0,8},{8,16},{16,24},{24,32},{32,40},{40,48},{48,56},{56,64},{64,7... | collective-permute-start | bytes 3128 | tf_op jit(solution)/shard_map/ppermute | solution.py:30
  384.3 4.3 collective-permute-start.18
  387.3 4.8 collective-permute-start.19
  392.3 7.0 collective-permute-start.20
  394.2 9.1 %collective-permute-start.21 = (f32[2,130,1]{2,1,0:T(8,128)S(1)}, f32[2,130,1]{2,1,0:T(8,128)S(1)}, u32[]{:S(2)}, u32[]{:S(2)}) collective-permute-start(f32[2,130,1]{2,1,0:T(8,128)S(1)} %get-tuple-element.327), channel_id=1, source_target_pairs={{0,8},{8,16},{16,24},{24,32},{32,40},{40,48},{48,56},{56,64},{64,7... | collective-permute-start | bytes 3128 | tf_op jit(solution)/shard_map/ppermute | solution.py:30
  412.1 59.3 %copy-start.38 = (f32[2,64,32]{1,2,0:T(8,128)}, f32[2,64,32]{1,2,0:T(8,128)S(1)}, u32[]{:S(2)}) copy-start(f32[2,64,32]{1,2,0:T(8,128)S(1)} %reduce_sum.92) | copy-start | bytes 49156
  413.0 5.2 collective-permute-start.22
  416.2 4.9 collective-permute-start.23
  421.1 5.9 collective-permute-start.24
  423.0 7.6 collective-permute-start.25
  430.9 30.9 %collective-permute-start.26 = (f32[2,1,32]{1,2,0:T(8,128)S(1)}, f32[2,1,32]{1,2,0:T(8,128)S(1)}, u32[]{:S(2)}, u32[]{:S(2)}) collective-permute-start(f32[2,1,32]{1,2,0:T(8,128)S(1)} %get-tuple-element.376), channel_id=1, source_target_pairs={{0,1},{1,2},{2,3},{3,4},{4,5},{5,6},{6,7},{8,9},{9,10},{10,11},{11... | collective-permute-start | bytes 776 | tf_op jit(solution)/shard_map/ppermute | solution.py:30
  434.3 27.5 %collective-permute-start.27 = (f32[2,1,32]{1,2,0:T(8,128)S(1)}, f32[2,1,32]{1,2,0:T(8,128)S(1)}, u32[]{:S(2)}, u32[]{:S(2)}) collective-permute-start(f32[2,1,32]{1,2,0:T(8,128)S(1)} %get-tuple-element.375), channel_id=1, source_target_pairs={{1,0},{2,1},{3,2},{4,3},{5,4},{6,5},{7,6},{9,8},{10,9},{11,10},{12... | collective-permute-start | bytes 776 | tf_op jit(solution)/shard_map/ppermute | solution.py:33
  461.7 108.2 %copy-start.4 = (f32[128,128]{1,0:T(8,128)}, f32[128,128]{1,0:T(8,128)S(1)}, u32[]{:S(2)}) copy-start(f32[128,128]{1,0:T(8,128)S(1)} %reduce_sum.97) | copy-start | bytes 196612
  461.9 5.9 collective-permute-start.28
  463.8 7.6 collective-permute-start.29
  661.8 59.3 %copy-start.12 = (f32[128,64]{1,0:T(8,128)S(1)}, f32[128,64]{1,0:T(8,128)}, u32[]{:S(2)}) copy-start(f32[128,64]{1,0:T(8,128)} %copy-done.11) | copy-start | bytes 98308
  662.2 58.8 %copy-start.7 = (f32[2,128,64]{2,1,0:T(8,128)S(1)}, f32[2,128,64]{2,1,0:T(8,128)}, u32[]{:S(2)}) copy-start(f32[2,128,64]{2,1,0:T(8,128)} %copy-done.6) | copy-start | bytes 196612
  662.3 59.0 %copy-start.32 = (f32[1,128,64]{2,1,0:T(8,128)S(1)}, f32[1,128,64]{2,1,0:T(8,128)}, u32[]{:S(2)}) copy-start(f32[1,128,64]{2,1,0:T(8,128)} %copy-done.31) | copy-start | bytes 98308
  663.5 3.6 collective-permute-start.30
  665.8 3.5 collective-permute-start.31
  669.3 5.9 collective-permute-start.32
  673.3 7.6 collective-permute-start.33
  682.7 4.6 collective-permute-start.34
  686.0 4.0 collective-permute-start.35
  690.1 5.9 collective-permute-start.36
  692.0 7.6 collective-permute-start.37
  702.8 4.7 collective-permute-start.38
  706.2 3.7 collective-permute-start.39
  710.0 7.0 collective-permute-start.40
  711.9 9.1 %collective-permute-start.41 = (f32[2,130,1]{2,1,0:T(8,128)S(1)}, f32[2,130,1]{2,1,0:T(8,128)S(1)}, u32[]{:S(2)}, u32[]{:S(2)}) collective-permute-start(f32[2,130,1]{2,1,0:T(8,128)S(1)} %get-tuple-element.325), channel_id=1, source_target_pairs={{0,8},{8,16},{16,24},{24,32},{32,40},{40,48},{48,56},{56,64},{64,7... | collective-permute-start | bytes 3128 | tf_op jit(solution)/shard_map/ppermute | solution.py:30
  721.4 4.6 collective-permute-start.42
  724.6 4.6 collective-permute-start.43
  729.4 7.0 collective-permute-start.44
  731.3 9.1 %collective-permute-start.45 = (f32[2,130,1]{2,1,0:T(8,128)S(1)}, f32[2,130,1]{2,1,0:T(8,128)S(1)}, u32[]{:S(2)}, u32[]{:S(2)}) collective-permute-start(f32[2,130,1]{2,1,0:T(8,128)S(1)} %get-tuple-element.323), channel_id=1, source_target_pairs={{0,8},{8,16},{16,24},{24,32},{32,40},{40,48},{48,56},{56,64},{64,7... | collective-permute-start | bytes 3128 | tf_op jit(solution)/shard_map/ppermute | solution.py:30
  741.3 4.5 collective-permute-start.46
  744.5 3.7 collective-permute-start.47
  748.3 9.8 %collective-permute-start.48 = (f32[2,258,1]{2,1,0:T(8,128)S(1)}, f32[2,258,1]{2,1,0:T(8,128)S(1)}, u32[]{:S(2)}, u32[]{:S(2)}) collective-permute-start(f32[2,258,1]{2,1,0:T(8,128)S(1)} %get-tuple-element.276), channel_id=1, source_target_pairs={{8,0},{16,8},{24,16},{32,24},{40,32},{48,40},{56,48},{64,56},{72,6... | collective-permute-start | bytes 6200 | tf_op jit(solution)/shard_map/ppermute | solution.py:33
  750.3 11.9 %collective-permute-start.49 = (f32[2,258,1]{2,1,0:T(8,128)S(1)}, f32[2,258,1]{2,1,0:T(8,128)S(1)}, u32[]{:S(2)}, u32[]{:S(2)}) collective-permute-start(f32[2,258,1]{2,1,0:T(8,128)S(1)} %get-tuple-element.277), channel_id=1, source_target_pairs={{0,8},{8,16},{16,24},{24,32},{32,40},{40,48},{48,56},{56,64},{64,7... | collective-permute-start | bytes 6200 | tf_op jit(solution)/shard_map/ppermute | solution.py:30
  762.7 4.5 collective-permute-start.50
  765.8 3.7 collective-permute-start.51
  769.8 9.9 %collective-permute-start.52 = (f32[2,258,1]{2,1,0:T(8,128)S(1)}, f32[2,258,1]{2,1,0:T(8,128)S(1)}, u32[]{:S(2)}, u32[]{:S(2)}) collective-permute-start(f32[2,258,1]{2,1,0:T(8,128)S(1)} %get-tuple-element.274), channel_id=1, source_target_pairs={{8,0},{16,8},{24,16},{32,24},{40,32},{48,40},{56,48},{64,56},{72,6... | collective-permute-start | bytes 6200 | tf_op jit(solution)/shard_map/ppermute | solution.py:33
  771.8 11.9 %collective-permute-start.53 = (f32[2,258,1]{2,1,0:T(8,128)S(1)}, f32[2,258,1]{2,1,0:T(8,128)S(1)}, u32[]{:S(2)}, u32[]{:S(2)}) collective-permute-start(f32[2,258,1]{2,1,0:T(8,128)S(1)} %get-tuple-element.275), channel_id=1, source_target_pairs={{0,8},{8,16},{16,24},{24,32},{32,40},{40,48},{48,56},{56,64},{64,7... | collective-permute-start | bytes 6200 | tf_op jit(solution)/shard_map/ppermute | solution.py:30
  785.1 12.2 %all-to-all-start = ((f32[2,128,256]{2,0,1:T(2,128)}), f32[2,128,256]{2,0,1:T(2,128)S(1)}, u32[]{:S(2)}, u32[]{:S(2)}) async-start(f32[2,128,256]{2,0,1:T(2,128)} %copy.728), calls=%async_computation | async-start | bytes 524288 | tf_op jit(solution)/shard_map/all_to_all | solution.py:178
  (70 other events, 1890.1 us)
where the time goes:
time: 835 us; the launch traced here: 820 us
  local copies, waits for them, and re-layouts  248 us (30%)
  other arithmetic  179 us (21%)
  blocking collectives  146 us (17%)
  starting transfers between devices  144 us (17%)
  waiting for transfers between devices  99.4 us (12%)
    ppermute x24, starting transfers between devices, padded_2(): lax.ppermute(lax.slice_in_dim(block, block.shape[dim] - width, None, axis...  76.4 us
    reshape x5, local copies, waits for them, and re-layouts, restrict(): return field.reshape(2, rows // 2, 2, cols // 2, 2).mean(axis=(2, 4))  72.1 us
    ppermute x24, waiting for transfers between devices, padded_2(): lax.ppermute(lax.slice_in_dim(block, block.shape[dim] - width, None, axis...  47.5 us
    ppermute x24, waiting for transfers between devices, padded_2(): lax.ppermute(lax.slice_in_dim(block, 0, width, axis=dim), axis, backward)  45.1 us
    ppermute x24, starting transfers between devices, padded_2(): lax.ppermute(lax.slice_in_dim(block, 0, width, axis=dim), axis, backward)  43.1 us
    reduce_sum x5, other arithmetic, restrict(): return field.reshape(2, rows // 2, 2, cols // 2, 2).mean(axis=(2, 4))  30.8 us
    reshape x2, local copies, waits for them, and re-layouts, coarsen(): east_four = east.reshape(rows // 2, 2, cols // 2, 2)  28.6 us
    reshape x2, local copies, waits for them, and re-layouts, coarsen(): spin_next = spin.reshape(rows // 2, 2, cols // 2, 2).mean(axis=(1, 3)) * 0.5  28 us
  transfers between devices with their start and end apart: 55, of which 30 were waited for; matrix products, arithmetic and copies ran while one was open for 29% of the time, Pallas kernels for 0%

commit v1 on v0

v1 whole, which is shorter than its diff:
```python
import math

import jax
import jax.numpy as jnp
from jax import lax
from jax.experimental import pallas as pl
from jax.experimental.pallas import tpu as pltpu
from jax.sharding import PartitionSpec as P

MESH = pl.DeviceIdType.MESH
GX, GY = 16, 8
OTILES = 16
MASS = 0.001
RELAX = 0.7
KEEP = 1.0 - RELAX
COS = math.cos(0.42)
SIN = math.sin(0.42)
SWEEPS = 16

B0, B1, FF, OC, NN, EE = range(6)
BASE = [0, 21, 42, 63, 84, 105]
FIRST = [118, 118, 118, 118, 118, 117]
TOP, OWN, BOT, END = 8, 24, 280, 296
NEIGHBOURS = [(dx, dy) for dy in (-1, 0, 1) for dx in (-1, 0, 1) if (dx, dy) != (0, 0)]


def lane_of(n):
    return lax.broadcasted_iota(jnp.int32, (n, 128), 1)


def row_of(n):
    return lax.broadcasted_iota(jnp.int32, (n, 128), 0)


def roll(x, k):
    return pltpu.roll(x, k % 128, 1)


def take(x, idx):
    return jnp.take_along_axis(x, idx, axis=1, mode="promise_in_bounds")


def within(v, lo, hi):
    return jnp.logical_and(v >= lo, v < hi)


def from_west(vals, s):
    if len(vals) == 1:
        return [roll(vals[0], s)]
    a, b = roll(vals[0], 1), roll(vals[1], 1)
    edge = lane_of(a.shape[0]) == 0
    return [jnp.where(edge, b, a), jnp.where(edge, a, b)]


def from_east(vals, s):
    if len(vals) == 1:
        return [roll(vals[0], -s)]
    a, b = roll(vals[0], -1), roll(vals[1], -1)
    edge = lane_of(a.shape[0]) == 127
    return [jnp.where(edge, b, a), jnp.where(edge, a, b)]


class Level:
    def __init__(self, tiles, rows, shift, b, e, n, f, d, pd, pf, x, y, res, chunk):
        self.tiles, self.rows, self.shift = tiles, rows, shift
        self.b, self.e, self.n, self.f = b, e, n, f
        self.d, self.pd, self.pf = d, pd, pf
        self.x, self.y, self.res, self.chunk = x, y, res, chunk

    def chunks(self, lo=None, hi=None):
        lo = 8 if lo is None else lo
        hi = 8 + self.rows if hi is None else hi
        while lo < hi:
            n = min(self.chunk, hi - lo)
            yield lo, n
            lo += n

    def setup(self, mask, r, n):
        ts = range(self.tiles)
        e = [self.e(t, r, n) for t in ts]
        w = from_west(e, self.shift)
        out = []
        for t in ts:
            f = self.f(t, r, n)
            d = MASS + e[t] + w[t] + self.n(t, r, n) + self.n(t, r - 1, n)
            g = RELAX / (d * d + f * f)
            m = mask(t, r, n)
            pd, pf = jnp.where(m, g * d, 0.0), jnp.where(m, g * f, 0.0)
            self.d[t, pl.ds(r, n), :] = d
            self.pd[t, pl.ds(r, n), :] = pd
            self.pf[t, pl.ds(r, n), :] = pf
            out.append((pd, pf))
        return out

    def start(self, r, n, given=None):
        for t in range(self.tiles):
            if given is None:
                pd, pf = self.pd[t, pl.ds(r, n), :], self.pf[t, pl.ds(r, n), :]
            else:
                pd, pf = given[t]
            b0, b1 = self.b(t, 0, r, n), self.b(t, 1, r, n)
            self.x[t, 0, pl.ds(r, n), :] = pd * b0 + pf * b1
            self.x[t, 1, pl.ds(r, n), :] = pd * b1 - pf * b0

    def around(self, src, r, n):
        ts = range(self.tiles)
        e = [self.e(t, r, n) for t in ts]
        north = [self.n(t, r, n) for t in ts]
        south = [self.n(t, r - 1, n) for t in ts]
        sums, xs = [], []
        for c in range(2):
            x = [src[t, c, pl.ds(r, n), :] for t in ts]
            xe = from_east(x, self.shift)
            xw = from_west([e[t] * x[t] for t in ts], self.shift)
            sums.append(
                [
                    (self.b(t, c, r, n) + e[t] * xe[t])
                    + (xw[t] + north[t] * src[t, c, pl.ds(r + 1, n), :])
                    + south[t] * src[t, c, pl.ds(r - 1, n), :]
                    for t in ts
                ]
            )
            xs.append(x)
        return sums, xs

    def relaxed(self, src, r, n, tiles=None):
        sums, xs = self.around(src, r, n)
        out = []
        for t in range(self.tiles if tiles is None else tiles):
            pd, pf = self.pd[t, pl.ds(r, n), :], self.pf[t, pl.ds(r, n), :]
            out.append(
                (
                    KEEP * xs[0][t] + pd * sums[0][t] + pf * sums[1][t],
                    KEEP * xs[1][t] + pd * sums[1][t] - pf * sums[0][t],
                )
            )
        return out

    def sweep(self, src, dst, lo=None, hi=None):
        for r, n in self.chunks(lo, hi):
            new = self.relaxed(src, r, n)
            for t in range(self.tiles):
                dst[t, 0, pl.ds(r, n), :] = new[t][0]
                dst[t, 1, pl.ds(r, n), :] = new[t][1]

    def residual(self, src, mask=None):
        for r, n in self.chunks():
            sums, xs = self.around(src, r, n)
            for t in range(self.tiles):
                d, f = self.d[t, pl.ds(r, n), :], self.f(t, r, n)
                r0 = sums[0][t] - d * xs[0][t] + f * xs[1][t]
                r1 = sums[1][t] - d * xs[1][t] - f * xs[0][t]
                if mask is not None:
                    m = mask(t, r, n)
                    r0, r1 = r0 * m, r1 * m
                self.res[t, 0, pl.ds(r, n), :] = r0
                self.res[t, 1, pl.ds(r, n), :] = r1


def kernel(
    vel_h, res_h, east_h, north_h, cor_h, land_h, ocv_h, own_h, drag_s,
    vout_h, stress_h,
    p0, land, vel, ocv, owner, drag,
    x0, y0, d0, pd0, pf0, rr0,
    cbuf, mr, ml, got_l, got_r, corner,
    oc1, oc2, oc3, oc4, oc5,
    p2, g2, m2, gb2,
    l1c, l1b, l1w, x1, y1, rr1,
    l2c, l2b, l2w, x2, y2, rr2,
    l3c, l3b, l3w, x3, y3, rr3,
    l4c, l4b, l4w, x4, y4, rr4,
    g1c, s1c, c5, g1b, s1b, b5, w5, x5, y5,
    up, up5, vout, turned, ice, stress,
    lsem, ns_s, ns_r, ew_s, ew_r, co_s, co_r, p2_s, p2_r, b2_s, b2_r,
    c1_s, c1_r, c2_s, c2_r, b1_s, b1_r, bb_s, bb_r, at_s, at_r,
):
    gx, gy = lax.axis_index("gx"), lax.axis_index("gy")

    def at(dx, dy):
        return (lax.rem(gx + dx + GX, GX), lax.rem(gy + dy + GY, GY))

    sent = []

    def send(src, dst, s, r, dev):
        c = pltpu.make_async_remote_copy(
            src_ref=src, dst_ref=dst, send_sem=s, recv_sem=r, device_id=dev, device_id_type=MESH
        )
        c.start()
        sent.append(c)
        return c

    def load(src, dst, k):
        c = pltpu.make_async_copy(src, dst, lsem.at[k])
        c.start()
        return c

    loads = [
        load(res_h, p0.at[0, 0:2, OWN:BOT, :], 0),
        load(cor_h, p0.at[0, FF, OWN:BOT, :], 1),
        load(north_h, p0.at[0, NN, OWN:BOT, :], 2),
        load(east_h, p0.at[0, EE, OWN:BOT, :], 3),
        load(land_h, land.at[OWN:BOT, :], 4),
    ]
    late = [load(own_h, owner, 5), load(ocv_h, ocv, 6), load(vel_h, vel, 7)]

    barrier = pltpu.get_barrier_semaphore()
    met = [at(dx, dy) for dx, dy in NEIGHBOURS]
    met += [at(o, 0) for o in range(2, GX - 1)] + [at(0, o) for o in range(2, GY - 1)]
    for dev in met:
        pl.semaphore_signal(barrier, inc=1, device_id=dev, device_id_type=MESH)

    zero = jnp.zeros((8, 128), jnp.float32)
    for t in range(2):
        p0[t, NN, 0:8, :] = zero
        for xx in (x0, y0):
            for c in range(2):
                xx[t, c, 0:8, :] = zero
                xx[t, c, END : END + 8, :] = zero
    for lc, xx, yy, rows in ((l1c, x1, y1, 144), (l2c, x2, y2, 128), (l3c, x3, y3, 64), (l4c, x4, y4, 32)):
        lc[1, 0:8, :] = zero
        for ref in (xx, yy):
            for c in range(2):
                ref[0, c, 0:8, :] = zero
                ref[0, c, 8 + rows : 16 + rows, :] = zero
    for ref in (x5, y5):
        for c in range(2):
            ref[c, 0:8, :] = zero
            ref[c, 72:80, :] = zero

    pl.semaphore_wait(barrier, len(met))

    rows_in = []
    for k, (src, dst) in enumerate(
        (
            (res_h, lambda a, b: p0.at[0, 0:2, a:b, :]),
            (cor_h, lambda a, b: p0.at[0, FF, a:b, :]),
            (north_h, lambda a, b: p0.at[0, NN, a:b, :]),
            (east_h, lambda a, b: p0.at[0, EE, a:b, :]),
            (land_h, lambda a, b: land.at[a:b, :]),
        )
    ):
        last = src.at[:, 240:256, :] if k == 0 else src.at[240:256, :]
        first = src.at[:, 0:16, :] if k == 0 else src.at[0:16, :]
        rows_in.append(send(last, dst(TOP, OWN), ns_s.at[2 * k], ns_r.at[2 * k], at(0, 1)))
        rows_in.append(send(first, dst(BOT, END), ns_s.at[2 * k + 1], ns_r.at[2 * k + 1], at(0, -1)))

    for c in loads:
        c.wait()

    def is_right(n):
        lane = lane_of(n)
        out = within(lane, 105, 116)
        for p in range(5):
            out = jnp.logical_or(out, within(lane, BASE[p], BASE[p] + 10))
        return out

    def is_left(n):
        lane = lane_of(n)
        out = within(lane, 116, 126)
        for p in range(5):
            out = jnp.logical_or(out, within(lane, BASE[p] + 10, BASE[p] + 20))
        return out

    for r in range(0, 256, 32):
        lane = lane_of(32)
        p0[0, OC, OWN + r : OWN + r + 32, :] = (1 - land[OWN + r : OWN + r + 32, :]).astype(jnp.float32)
        packed = roll(p0[0, EE, OWN + r : OWN + r + 32, :], BASE[EE] - FIRST[EE])
        for p in (NN, OC, FF, B1, B0):
            part = roll(p0[0, p, OWN + r : OWN + r + 32, :], BASE[p] - FIRST[p])
            packed = jnp.where(lane < BASE[p] + 21, part, packed)
        cbuf[r : r + 32, :] = packed
    for r in range(0, 128, 32):
        a, b = cbuf[r : r + 32, :], cbuf[128 + r : 160 + r, :]
        mr[r : r + 32, :] = jnp.where(is_right(32), a, roll(b, 11))
        ml[r : r + 32, :] = jnp.where(is_left(32), a, roll(b, -11))
    edge_in = [
        send(mr, got_l, ew_s.at[0], ew_r.at[0], at(1, 0)),
        send(ml, got_r, ew_s.at[1], ew_r.at[1], at(-1, 0)),
        send(cbuf.at[240:256, :], corner.at[0], co_s.at[0], co_r.at[0], at(1, 1)),
        send(cbuf.at[240:256, :], corner.at[1], co_s.at[1], co_r.at[1], at(-1, 1)),
        send(cbuf.at[0:16, :], corner.at[2], co_s.at[2], co_r.at[2], at(1, -1)),
        send(cbuf.at[0:16, :], corner.at[3], co_s.at[3], co_r.at[3], at(-1, -1)),
    ]

    def thinned(load_e, load_n, load_f, n):
        e = (load_e(0) + load_e(1)) * 0.25
        no = load_n(1)
        f = load_f(0) + load_f(1)
        return e, (no + roll(no, -1)) * 0.25, (f + roll(f, -1)) * 0.125

    def own_coarse(src, dst, rows):
        n = min(rows, 32)
        for r in range(0, rows, n):
            idx = (2 * lane_of(n)) & 127
            e, no, f = thinned(*(lambda odd, p=p: src(p, 2 * r + odd, n) for p in range(3)), n)
            dst[0, r : r + n, :] = take(e, idx + 1)
            dst[1, r : r + n, :] = take(no, idx)
            dst[2, r : r + n, :] = take(f, idx)

    own_coarse(lambda p, r, n: p0[0, (EE, NN, FF)[p], pl.ds(OWN + r, n, 2), :], oc1, 128)
    for src, dst, rows in ((oc1, oc2, 64), (oc2, oc3, 32), (oc3, oc4, 16), (oc4, oc5, 8)):
        own_coarse(lambda p, r, n, src=src: src[p, pl.ds(r, n, 2), :], dst, rows)

    lane = lane_of(64)
    p2[...] = jnp.where(
        lane < 32, oc2[0], jnp.where(lane < 64, roll(oc2[1], 32), roll(oc2[2], 64))
    )
    coef_in = []
    for k, (dx, dy) in enumerate(NEIGHBOURS):
        if dy == 0:
            src, dst = p2, g2.at[1 - dx, 32:96, :]
        elif dy == 1:
            src, dst = p2.at[32:64, :], g2.at[1 - dx, 0:32, :]
        else:
            src, dst = p2.at[0:32, :], g2.at[1 - dx, 96:128, :]
        coef_in.append(send(src, dst, p2_s.at[k], p2_r.at[k], at(dx, dy)))
    g2[1, 32:96, :] = p2[...]

    lane = lane_of(8)
    place = (lane - 4 * gx) & 63
    idx5 = jnp.where(place < 4, place, 0)
    here0 = jnp.logical_and(place < 4, lane < 64)
    here1 = jnp.logical_and(place < 4, lane >= 64)
    e5, n5, f5 = (take(oc5[p], idx5) for p in range(3))
    g1c[0, 0] = jnp.where(here0, e5, jnp.where(here1, n5, 0.0))
    g1c[0, 1] = jnp.where(here0, f5, 0.0)
    gat_c = [
        send(g1c.at[0], g1c.at[o], c1_s.at[o - 1], c1_r.at[o - 1], at(o, 0)) for o in range(1, GX)
    ]

    for c in late:
        c.wait()
    tiles = [drag_s[k] for k in range(OTILES)]
    for j in range(0, 2048, 512):
        ow = owner[:, j : j + 512]
        dr = jnp.zeros((16, 512), jnp.float32)
        for k in range(OTILES):
            dr = jnp.where(ow == k, tiles[k], dr)
        drag[:, j : j + 512] = dr

    for c in rows_in + edge_in:
        c.wait_recv()

    def spread(packed, r):
        lane, row = lane_of(16), row_of(16) + (r - OWN)
        col = jnp.where(lane < 64, lane + 128, lane - 128) + 128 * gx
        inside = jnp.logical_and(within(col, 0, 128 * GX), within(row + 256 * gy, 0, 256 * GY))
        near = jnp.logical_or(lane < 10, lane >= 118)
        for p in range(6):
            v = roll(packed, FIRST[p] - BASE[p])
            if p == OC:
                v = jnp.where(jnp.logical_and(inside, near), v, 0.0)
            elif p in (NN, EE):
                v = jnp.where(inside, v, 0.0)
            p0[1, p, r : r + 16, :] = v

    right = is_right(16)
    for r in range(0, 128, 16):
        a, b = got_l[r : r + 16, :], got_r[r : r + 16, :]
        spread(jnp.where(right, a, b), OWN + r)
        spread(jnp.where(right, roll(a, -11), roll(b, 11)), OWN + 128 + r)
    spread(jnp.where(right, corner[0], corner[1]), TOP)
    spread(jnp.where(right, corner[2], corner[3]), BOT)
    for r, there in ((TOP, gy > 0), (BOT, gy < GY - 1)):
        keep = jnp.where(there, 1.0, 0.0)
        p0[0, OC, r : r + 16, :] = (1 - land[r : r + 16, :]).astype(jnp.float32) * keep
        p0[0, NN, r : r + 16, :] = p0[0, NN, r : r + 16, :] * keep

    fine = Level(
        2, 288, 1,
        lambda t, c, r, n: p0[t, c, pl.ds(r, n), :],
        lambda t, r, n: p0[t, EE, pl.ds(r, n), :],
        lambda t, r, n: p0[t, NN, pl.ds(r, n), :],
        lambda t, r, n: p0[t, FF, pl.ds(r, n), :],
        d0, pd0, pf0, x0, y0, rr0, 32,
    )

    def ocean(t, r, n):
        return p0[t, OC, pl.ds(r, n), :]

    for r, n in fine.chunks():
        fine.start(r, n, fine.setup(lambda t, r, n: ocean(t, r, n) > 0.5, r, n))
    fine.sweep(x0, y0)
    fine.residual(y0, ocean)

    def single(lc, lb, lw, x, y, rr, rows, shift, chunk):
        return Level(
            1, rows, shift,
            lambda t, c, r, n: lb[c, pl.ds(r, n), :],
            lambda t, r, n: lc[0, pl.ds(r, n), :],
            lambda t, r, n: lc[1, pl.ds(r, n), :],
            lambda t, r, n: lc[2, pl.ds(r, n), :],
            lw.at[0:1], lw.at[1:2], lw.at[2:3], x, y, rr, chunk,
        )

    one = single(l1c, l1b, l1w, x1, y1, rr1, 144, 1, 48)
    for r in range(0, 144, 48):
        n = 48
        idx = (2 * lane_of(n)) & 127
        low = lane_of(n) < 64

        def pick(pair, odd):
            return jnp.where(low, take(pair[0], idx + odd), take(pair[1], idx + odd))

        parts = [
            thinned(
                *(lambda odd, p=p, t=t: p0[t, p, pl.ds(TOP + 2 * r + odd, n, 2), :] for p in (EE, NN, FF)), n
            )
            for t in range(2)
        ]
        for p in range(3):
            l1c[p, 8 + r : 8 + r + n, :] = pick([parts[0][p], parts[1][p]], 1 if p == 0 else 0)
        for c in range(2):
            pair = []
            for t in range(2):
                v = rr0[t, c, pl.ds(TOP + 2 * r, n, 2), :] + rr0[t, c, pl.ds(TOP + 2 * r + 1, n, 2), :]
                pair.append((v + roll(v, -1)) * 0.25)
            l1b[c, 8 + r : 8 + r + n, :] = pick(pair, 0)

    def mask1(t, r, n):
        lane = lane_of(n)
        col = jnp.where(lane < 96, lane, lane - 128) + 64 * gx
        row = row_of(n) + (r - 16) + 128 * gy
        return jnp.logical_and(within(col, 0, 64 * GX), within(row, 0, 128 * GY))

    for r, n in one.chunks():
        one.start(r, n, one.setup(mask1, r, n))
    one.sweep(x1, y1)
    one.residual(y1)

    halves = []
    for half in range(2):
        n = 32
        idx = (2 * lane_of(n)) & 127
        for c in range(2):
            r = 16 + 64 * half
            v = rr1[0, c, pl.ds(r, n, 2), :] + rr1[0, c, pl.ds(r + 1, n, 2), :]
            halves.append(take((v + roll(v, -1)) * 0.25, idx))
    lane = lane_of(32)
    m2[...] = jnp.where(
        lane < 64,
        jnp.where(lane < 32, halves[0], roll(halves[1], 32)),
        jnp.where(lane < 96, roll(halves[2], 64), roll(halves[3], 96)),
    )
    res_in = []
    for k, (dx, dy) in enumerate(NEIGHBOURS):
        res_in.append(send(m2, gb2.at[1 - dy, 1 - dx], b2_s.at[k], b2_r.at[k], at(dx, dy)))

    for c in coef_in:
        c.wait_recv()
    for r in range(0, 128, 32):
        lane = lane_of(32)
        for p in range(3):
            left, mid, rite = (g2[k, r : r + 32, :] for k in range(3))
            v = jnp.where(lane < 32, roll(mid, -32 * p), roll(rite, 32 - 32 * p))
            col = jnp.where(lane < 64, lane, lane - 128) + 32 * gx
            row = row_of(32) + (r - 32) + 64 * gy
            ok = jnp.logical_and(within(col, 0, 32 * GX), within(row, 0, 64 * GY))
            ok = jnp.logical_and(ok, jnp.logical_or(lane < 64, lane >= 96))
            l2c[p, 8 + r : 40 + r, :] = jnp.where(ok, jnp.where(lane < 64, v, roll(left, 96 - 32 * p)), 0.0)

    def masker(own_rows, halo):
        def mask(t, r, n):
            lane = lane_of(n)
            col = jnp.where(lane < 64, lane, lane - 128) + 32 * gx
            row = row_of(n) + (r - 8 - halo) + own_rows * gy
            ok = jnp.logical_and(within(col, 0, 32 * GX), within(row, 0, own_rows * GY))
            return jnp.logical_and(ok, jnp.logical_or(lane < 64, lane >= 96))

        return mask

    def partner(x, s):
        return jnp.where((lane_of(x.shape[0]) & s) == 0, roll(x, -s), roll(x, s))

    def wide_coarse(src, dst, rows, s):
        ev = lambda p: src[p, pl.ds(8, rows, 2), :]
        od = lambda p: src[p, pl.ds(9, rows, 2), :]
        e = (ev(0) + od(0)) * 0.25
        dst[0, 8 : 8 + rows, :] = jnp.where((lane_of(rows) & s) == 0, roll(e, -s), e)
        no = od(1)
        dst[1, 8 : 8 + rows, :] = (no + partner(no, s)) * 0.25
        f = ev(2) + od(2)
        dst[2, 8 : 8 + rows, :] = (f + partner(f, s)) * 0.125

    wide_coarse(l2c, l3c, 64, 1)
    wide_coarse(l3c, l4c, 32, 2)
    two = single(l2c, l2b, l2w, x2, y2, rr2, 128, 1, 32)
    three = single(l3c, l3b, l3w, x3, y3, rr3, 64, 2, 32)
    four = single(l4c, l4b, l4w, x4, y4, rr4, 32, 4, 32)
    masks = {}
    for lev, own_rows, halo in ((two, 64, 32), (three, 32, 16), (four, 16, 8)):
        masks[lev] = masker(own_rows, halo)
        for r, n in lev.chunks():
            lev.setup(masks[lev], r, n)

    for c in gat_c:
        c.wait_recv()

    def total(g):
        parts = [g[k] for k in range(GX)]
        while len(parts) > 1:
            parts = [parts[i] + parts[i + 1] for i in range(0, len(parts), 2)]
        return parts[0]

    mine = pl.ds(pl.multiple_of(8 * gy, 8), 8)
    s1c[...] = total(g1c)
    c5[:, mine, :] = s1c[...]
    gat_c2 = [
        send(s1c, c5.at[:, mine, :], c2_s.at[o - 1], c2_r.at[o - 1], at(0, o)) for o in range(1, GY)
    ]

    for c in res_in:
        c.wait_recv()
    gb2[1, 1] = m2[...]
    lane = lane_of(32)
    for q, (dy, half) in enumerate(((0, 1), (1, 0), (1, 1), (2, 0))):
        for c in range(2):
            o = 64 * half + 32 * c
            left, mid, rite = (gb2[dy, k] for k in range(3))
            v = jnp.where(lane < 32, roll(mid, -o), roll(rite, 32 - o))
            v = jnp.where(lane < 64, v, roll(left, 96 - o))
            l2b[c, 8 + 32 * q : 40 + 32 * q, :] = v

    def restricted(src, dst, rows, s):
        for c in range(2):
            v = src[0, c, pl.ds(8, rows, 2), :] + src[0, c, pl.ds(9, rows, 2), :]
            dst[c, 8 : 8 + rows, :] = (v + partner(v, s)) * 0.25

    for lev in (two, three, four):
        for r, n in lev.chunks():
            lev.start(r, n)
        lev.sweep(lev.x, lev.y)
        lev.residual(lev.y)
        if lev is two:
            restricted(rr2, l3b, 64, 1)
        if lev is three:
            restricted(rr3, l4b, 32, 2)

    lane = lane_of(8)
    u = []
    for c in range(2):
        v = rr4[0, c, pl.ds(16, 8, 2), :] + rr4[0, c, pl.ds(17, 8, 2), :]
        u.append(take((v + roll(v, -4)) * 0.25, 8 * idx5))
    g1b[0] = jnp.where(here0, u[0], jnp.where(here1, u[1], 0.0))
    gat_b = [
        send(g1b.at[0], g1b.at[o], b1_s.at[o - 1], b1_r.at[o - 1], at(o, 0)) for o in range(1, GX)
    ]
    for c in gat_c2:
        c.wait_recv()
    n = 64
    lane, row = lane_of(n), row_of(n)
    first = lane < 64

    def both(v):
        return jnp.where(first, v, roll(v, 64))

    en = c5[0]
    e5, n5, f5 = both(en), both(roll(en, 64)), both(c5[1])
    col = lane & 63
    ecut = jnp.where(col == 63, 0.0, e5)
    wcut = jnp.where(col == 0, 0.0, roll(e5, 1))
    w5[0, 0:8, :] = zero
    w5[0, 8:72, :] = n5
    s5 = w5[0, 7:71, :]
    diag = MASS + e5 + wcut + n5 + s5
    g = RELAX / (diag * diag + f5 * f5)
    pd5 = g * diag
    pf5 = jnp.where(first, g * f5, -(g * f5))

    for c in gat_b:
        c.wait_recv()
    s1b[...] = total(g1b)
    b5[mine, :] = s1b[...]
    gat_b2 = [
        send(s1b, b5.at[mine, :], bb_s.at[o - 1], bb_r.at[o - 1], at(0, o)) for o in range(1, GY)
    ]
    w5[1, 8:72, :] = ecut
    w5[2, 8:72, :] = wcut
    w5[3, 8:72, :] = s5
    w5[4, 8:72, :] = pd5
    w5[5, 8:72, :] = pf5
    for c in gat_b2:
        c.wait_recv()
    rhs = b5[...]
    other = roll(rhs, 64)
    x5[0, 8:72, :] = w5[4, 8:72, :] * rhs + w5[5, 8:72, :] * other
    x5[1, 8:72, :] = w5[4, 8:72, :] * other - w5[5, 8:72, :] * rhs
    w5[6, 8:72, :] = other
    here, there = x5, y5
    for _ in range(SWEEPS - 1):
        t = []
        for c in range(2):
            x = here[c, 8:72, :]
            t.append(
                ((b5[...] if c == 0 else w5[6, 8:72, :]) + w5[1, 8:72, :] * roll(x, -1))
                + (w5[2, 8:72, :] * roll(x, 1) + w5[0, 8:72, :] * here[c, 9:73, :])
                + w5[3, 8:72, :] * here[c, 7:71, :]
            )
        there[0, 8:72, :] = KEEP * here[0, 8:72, :] + w5[4, 8:72, :] * t[0] + w5[5, 8:72, :] * t[1]
        there[1, 8:72, :] = KEEP * here[1, 8:72, :] + w5[4, 8:72, :] * t[1] - w5[5, 8:72, :] * t[0]
        here, there = there, here

    near = here[0, pl.ds(pl.multiple_of(8 * gy, 8), 24), :]
    lane = lane_of(24)
    col = 4 * gx + (jnp.where(lane < 64, lane, lane - 128) >> 3)
    idx = jnp.clip(col, 0, 63)
    for c in range(2):
        up5[c] = take(near, idx + 64 * c)
    for c in range(2):
        v = up5[c, 4:20, :]
        up[0, c, pl.ds(8, 16, 2), :] = v
        up[0, c, pl.ds(9, 16, 2), :] = v
        y4[0, c, 8:40, :] = y4[0, c, 8:40, :] + jnp.where(masks[four](0, 8, 32), up[0, c, 8:40, :], 0.0)
    four.sweep(y4, x4)
    four.sweep(x4, y4)

    for lev, coarse, rows in ((three, y4, 64), (two, y3, 128)):
        for c in range(2):
            v = coarse[0, c, 8 : 8 + rows // 2, :]
            up[0, c, pl.ds(8, rows // 2, 2), :] = v
            up[0, c, pl.ds(9, rows // 2, 2), :] = v
            lev.y[0, c, 8 : 8 + rows, :] = lev.y[0, c, 8 : 8 + rows, :] + up[0, c, 8 : 8 + rows, :]
        lev.sweep(lev.y, lev.x)
        lev.sweep(lev.x, lev.y)

    lane = lane_of(72)
    idx = jnp.where(lane < 96, lane >> 1, (lane >> 1) + 64)
    for c in range(2):
        v = take(y2[0, c, 36:108, :], idx)
        up[0, c, pl.ds(8, 72, 2), :] = v
        up[0, c, pl.ds(9, 72, 2), :] = v
        y1[0, c, 8:152, :] = y1[0, c, 8:152, :] + up[0, c, 8:152, :]
    one.sweep(y1, x1)
    one.sweep(x1, y1)

    for r in range(0, 144, 48):
        idx = lane_of(48) >> 1
        for c in range(2):
            v = y1[0, c, 8 + r : 56 + r, :]
            for t in range(2):
                w = take(v, idx + 64 * t)
                up[t, c, pl.ds(8 + 2 * r, 48, 2), :] = w
                up[t, c, pl.ds(9 + 2 * r, 48, 2), :] = w
    for r, n in fine.chunks():
        for t in range(2):
            m = ocean(t, r, n)
            for c in range(2):
                y0[t, c, pl.ds(r, n), :] = y0[t, c, pl.ds(r, n), :] + m * up[t, c, pl.ds(r, n), :]
    fine.sweep(y0, x0, 16, 288)

    ice_in = []
    out_copies = []
    for h in range(2):
        for r in range(128 * h, 128 * h + 128, 32):
            new = fine.relaxed(x0, OWN + r, 32, 1)[0]
            for c in range(2):
                vout[c, r : r + 32, :] = vel[c, r : r + 32, :] + new[c]
        for c in range(2):
            turned[c, :, 128 * h : 128 * h + 128] = vout[c, 128 * h : 128 * h + 128, :].T
        lanes = pl.ds(pl.multiple_of(256 * gy + 128 * h, 128), 128)
        for o in range(1, GY):
            dev = at(0, o)
            k = 7 * h + o - 1
            ice_in.append(
                send(
                    turned.at[:, pl.ds(pl.multiple_of(16 * dev[1], 16), 16), 128 * h : 128 * h + 128],
                    ice.at[:, :, lanes],
                    at_s.at[k], at_r.at[k], dev,
                )
            )
        ice[:, :, lanes] = turned[:, pl.ds(pl.multiple_of(16 * gy, 16), 16), 128 * h : 128 * h + 128]
    out = pltpu.make_async_copy(vout, vout_h, lsem.at[0])
    out.start()
    out_copies.append(out)
    for c in ice_in:
        c.wait_recv()
    for j in range(0, 2048, 512):
        s = slice(j, j + 512)
        a, b = ice[0, :, s] - ocv[0, :, s], ice[1, :, s] - ocv[1, :, s]
        scale = drag[:, s] * jnp.sqrt(a * a + b * b)
        stress[0, :, s] = scale * (COS * a - SIN * b)
        stress[1, :, s] = scale * (SIN * a + COS * b)
    out = pltpu.make_async_copy(stress, stress_h, lsem.at[1])
    out.start()
    out_copies.append(out)
    for c in sent:
        c.wait_send()
    for c in out_copies:
        c.wait()


def on_device(velocity, residual, east, north, coriolis, land, ocean_velocity, owner, tile_drag):
    f32 = jnp.float32

    def vm(*shape, dtype=f32):
        return pltpu.VMEM(shape, dtype)

    def level(rows):
        n = rows + 16
        return [vm(3, n, 128), vm(2, n, 128), vm(3, n, 128), vm(1, 2, n, 128), vm(1, 2, n, 128), vm(1, 2, n, 128)]

    scratch = [
        vm(2, 6, 304, 128), vm(304, 128, dtype=jnp.int32), vm(2, 256, 128), vm(2, 16, 2048),
        vm(16, 2048, dtype=jnp.int32), vm(16, 2048),
        vm(2, 2, 304, 128), vm(2, 2, 304, 128), vm(2, 304, 128), vm(2, 304, 128), vm(2, 304, 128),
        vm(2, 2, 304, 128),
        vm(256, 128), vm(128, 128), vm(128, 128), vm(128, 128), vm(128, 128), vm(4, 16, 128),
        vm(3, 128, 128), vm(3, 64, 128), vm(3, 32, 128), vm(3, 16, 128), vm(3, 8, 128),
        vm(64, 128), vm(3, 128, 128), vm(32, 128), vm(3, 3, 32, 128),
        *level(144), *level(128), *level(64), *level(32),
        vm(16, 2, 8, 128), vm(2, 8, 128), vm(2, 64, 128), vm(16, 8, 128), vm(8, 128), vm(64, 128),
        vm(7, 80, 128), vm(2, 80, 128), vm(2, 80, 128),
        vm(2, 2, 304, 128), vm(2, 24, 128), vm(2, 256, 128), vm(2, 128, 256), vm(2, 16, 2048), vm(2, 16, 2048),
        pltpu.SemaphoreType.DMA((8,)),
    ]
    for count in (10, 2, 4, 8, 8, 15, 7, 15, 7, 14):
        scratch += [pltpu.SemaphoreType.DMA((count,))] * 2
    hbm = pl.BlockSpec(memory_space=pl.ANY)
    return pl.pallas_call(
        kernel,
        out_shape=(
            jax.ShapeDtypeStruct((2, 256, 128), f32),
            jax.ShapeDtypeStruct((2, 16, 2048), f32),
        ),
        in_specs=[hbm] * 8 + [pl.BlockSpec(memory_space=pltpu.SMEM)],
        out_specs=(hbm, hbm),
        scratch_shapes=scratch,
        compiler_params=pltpu.CompilerParams(
            collective_id=0, has_side_effects=True, vmem_limit_bytes=48 * 1024 * 1024
        ),
    )(velocity, residual, east, north, coriolis, land, ocean_velocity, owner, tile_drag)


def solution(mesh):
    placed = (
        P(None, "gy", "gx"),
        P(None, "gy", "gx"),
        P("gy", "gx"),
        P("gy", "gx"),
        P("gy", "gx"),
        P("gy", "gx"),
        P(None, ("gx", "gy"), None),
        P(("gx", "gy"), None),
        P(),
    )
    return jax.shard_map(
        on_device,
        mesh=mesh,
        in_specs=placed,
        out_specs=(P(None, "gy", "gx"), P(None, ("gx", "gy"), None)),
        check_vma=False,
    )
```

time: 835 us -> 54.2 us (0.06)
  the two profiles are of different devices: /device:TPU:32 before, /device:TPU:1 now
where the time goes in v1:
time: 54.2 us; the launch traced here: 53.9 us
  Pallas kernels  43.8 us (81%)
  local copies, waits for them, and re-layouts  9.42 us (17%)
  between operations  0.66 us (1%)
    pallas_call x1, Pallas kernels, on_device(): pl.pallas_call(kernel, out_shape=(jax.ShapeDtypeStruct((2, 256, 128), f32...  43.8 us
    unnamed x20, local copies, waits for them, and re-layouts  9.42 us

profile of v1, /device:TPU:1, one launch (start us, length us, event | category | flops | bytes accessed | tf_op | source)
XLA Modules:
  0.0 53.9 jit_solution(11977945763674026351)
XLA Ops:
  0.6 0.0 copy-start
  0.6 0.9 %copy-done = f32[2,256,128]{2,1,0:T(8,128)S(1)} copy-done((f32[2,256,128]{2,1,0:T(8,128)S(1)}, f32[2,256,128]{2,1,0:T(8,128)}, u32[]{:S(2)}) %copy-start) | copy-done | bytes 262168
  1.6 0.0 copy-start.1
  1.6 0.9 %copy-done.1 = f32[2,256,128]{2,1,0:T(8,128)S(1)} copy-done((f32[2,256,128]{2,1,0:T(8,128)S(1)}, f32[2,256,128]{2,1,0:T(8,128)}, u32[]{:S(2)}) %copy-start.1) | copy-done | bytes 262168
  2.5 0.0 copy-start.2
  2.5 0.9 %copy-done.2 = f32[2,16,2048]{2,1,0:T(8,128)S(1)} copy-done((f32[2,16,2048]{2,1,0:T(8,128)S(1)}, f32[2,16,2048]{2,1,0:T(8,128)}, u32[]{:S(2)}) %copy-start.2) | copy-done | bytes 262168
  3.5 0.0 copy-start.3
  3.5 0.9 %copy-done.3 = f32[256,128]{1,0:T(8,128)S(1)} copy-done((f32[256,128]{1,0:T(8,128)S(1)}, f32[256,128]{1,0:T(8,128)}, u32[]{:S(2)}) %copy-start.3) | copy-done | bytes 131096
  4.4 0.0 copy-start.4
  4.4 0.9 %copy-done.4 = f32[256,128]{1,0:T(8,128)S(1)} copy-done((f32[256,128]{1,0:T(8,128)S(1)}, f32[256,128]{1,0:T(8,128)}, u32[]{:S(2)}) %copy-start.4) | copy-done | bytes 131096
  5.3 0.0 copy-start.5
  5.3 0.9 %copy-done.5 = f32[256,128]{1,0:T(8,128)S(1)} copy-done((f32[256,128]{1,0:T(8,128)S(1)}, f32[256,128]{1,0:T(8,128)}, u32[]{:S(2)}) %copy-start.5) | copy-done | bytes 131096
  6.2 0.0 copy-start.6
  6.2 0.9 %copy-done.6 = s32[256,128]{1,0:T(8,128)S(1)} copy-done((s32[256,128]{1,0:T(8,128)S(1)}, s32[256,128]{1,0:T(8,128)}, u32[]{:S(2)}) %copy-start.6) | copy-done | bytes 131096
  7.1 0.0 copy-start.7
  7.1 0.9 %copy-done.7 = s32[16,2048]{1,0:T(8,128)S(1)} copy-done((s32[16,2048]{1,0:T(8,128)S(1)}, s32[16,2048]{1,0:T(8,128)}, u32[]{:S(2)}) %copy-start.7) | copy-done | bytes 131096
  8.0 0.0 copy-start.8
  8.0 0.7 %copy-done.8 = f32[16]{0:T(128)S(1)} copy-done((f32[16]{0:T(128)S(1)}, f32[16]{0:T(128)}, u32[]{:S(2)}) %copy-start.8) | copy-done | bytes 88
  8.7 43.8 %shard_map.104 = (f32[2,256,128]{2,1,0:T(8,128)S(1)}, f32[2,16,2048]{2,1,0:T(8,128)S(1)}) custom-call(f32[2,256,128]{2,1,0:T(8,128)S(1)} %copy-done, f32[2,256,128]{2,1,0:T(8,128)S(1)} %copy-done.1, f32[256,128]{1,0:T(8,128)S(1)} %copy-done.3, f32[256,128]{1,0:T(8,128)S(1)} %copy-done.4, f32[256,128]{1,0:T(8,128)S(1)} %copy-done.5, ...), custom_call_target="tpu_custom_call" | custom-call | tf_op jit(solution)/shard_map/pallas_call | solution.py:719
  52.5 0.7 %copy.13 = f32[2,256,128]{2,1,0:T(8,128)} copy(f32[2,256,128]{2,1,0:T(8,128)S(1)} %get-tuple-element.4) | data formatting | bytes 524288
  53.2 0.7 %copy.14 = f32[2,16,2048]{2,1,0:T(8,128)} copy(f32[2,16,2048]{2,1,0:T(8,128)S(1)} %get-tuple-element.5) | data formatting | bytes 524288
Async XLA Ops:
  0.6 1.0 %copy-start = (f32[2,256,128]{2,1,0:T(8,128)S(1)}, f32[2,256,128]{2,1,0:T(8,128)}, u32[]{:S(2)}) copy-start(f32[2,256,128]{2,1,0:T(8,128)} %vel_h.1) | copy-start | bytes 786436
  1.6 0.9 %copy-start.1 = (f32[2,256,128]{2,1,0:T(8,128)S(1)}, f32[2,256,128]{2,1,0:T(8,128)}, u32[]{:S(2)}) copy-start(f32[2,256,128]{2,1,0:T(8,128)} %res_h.1) | copy-start | bytes 786436
  2.5 0.9 %copy-start.2 = (f32[2,16,2048]{2,1,0:T(8,128)S(1)}, f32[2,16,2048]{2,1,0:T(8,128)}, u32[]{:S(2)}) copy-start(f32[2,16,2048]{2,1,0:T(8,128)} %ocv_h.1) | copy-start | bytes 786436
  3.5 0.9 %copy-start.3 = (f32[256,128]{1,0:T(8,128)S(1)}, f32[256,128]{1,0:T(8,128)}, u32[]{:S(2)}) copy-start(f32[256,128]{1,0:T(8,128)} %east_h.1) | copy-start | bytes 393220
  4.4 0.9 %copy-start.4 = (f32[256,128]{1,0:T(8,128)S(1)}, f32[256,128]{1,0:T(8,128)}, u32[]{:S(2)}) copy-start(f32[256,128]{1,0:T(8,128)} %north_h.1) | copy-start | bytes 393220
  5.3 0.9 %copy-start.5 = (f32[256,128]{1,0:T(8,128)S(1)}, f32[256,128]{1,0:T(8,128)}, u32[]{:S(2)}) copy-start(f32[256,128]{1,0:T(8,128)} %cor_h.1) | copy-start | bytes 393220
  6.2 0.9 %copy-start.6 = (s32[256,128]{1,0:T(8,128)S(1)}, s32[256,128]{1,0:T(8,128)}, u32[]{:S(2)}) copy-start(s32[256,128]{1,0:T(8,128)} %land_h.1) | copy-start | bytes 393220
  7.1 0.9 %copy-start.7 = (s32[16,2048]{1,0:T(8,128)S(1)}, s32[16,2048]{1,0:T(8,128)}, u32[]{:S(2)}) copy-start(s32[16,2048]{1,0:T(8,128)} %own_h.1) | copy-start | bytes 393220
  8.0 0.7 %copy-start.8 = (f32[16]{0:T(128)S(1)}, f32[16]{0:T(128)}, u32[]{:S(2)}) copy-start(f32[16]{0:T(128)} %drag_s.1) | copy-start | bytes 196

commit v2 on v1

--- a/solution.py
+++ b/solution.py
@@ -158,9 +158,9 @@
 
 
 def kernel(
-    vel_h, res_h, east_h, north_h, cor_h, land_h, ocv_h, own_h, drag_s,
-    vout_h, stress_h,
-    p0, land, vel, ocv, owner, drag,
+    vel_h, res_h, east_h, north_h, cor_h, land_h, ocv_h, own_h, drag_h,
+    vout, stress,
+    drag_s, p0, land, vel, ocv, owner, drag,
     x0, y0, d0, pd0, pf0, rr0,
     cbuf, mr, ml, got_l, got_r, corner,
     oc1, oc2, oc3, oc4, oc5,
@@ -170,7 +170,7 @@
     l3c, l3b, l3w, x3, y3, rr3,
     l4c, l4b, l4w, x4, y4, rr4,
     g1c, s1c, c5, g1b, s1b, b5, w5, x5, y5,
-    up, up5, vout, turned, ice, stress,
+    up, up5, turned, ice,
     lsem, ns_s, ns_r, ew_s, ew_r, co_s, co_r, p2_s, p2_r, b2_s, b2_r,
     c1_s, c1_r, c2_s, c2_r, b1_s, b1_r, bb_s, bb_r, at_s, at_r,
 ):
@@ -201,7 +201,7 @@
         load(east_h, p0.at[0, EE, OWN:BOT, :], 3),
         load(land_h, land.at[OWN:BOT, :], 4),
     ]
-    late = [load(own_h, owner, 5), load(ocv_h, ocv, 6), load(vel_h, vel, 7)]
+    late = [load(own_h, owner, 5), load(ocv_h, ocv, 6), load(vel_h, vel, 7), load(drag_h, drag_s, 8)]
 
     barrier = pltpu.get_barrier_semaphore()
     met = [at(dx, dy) for dx, dy in NEIGHBOURS]
@@ -649,7 +649,6 @@
     fine.sweep(y0, x0, 16, 288)
 
     ice_in = []
-    out_copies = []
     for h in range(2):
         for r in range(128 * h, 128 * h + 128, 32):
             new = fine.relaxed(x0, OWN + r, 32, 1)[0]
@@ -669,9 +668,6 @@
                 )
             )
         ice[:, :, lanes] = turned[:, pl.ds(pl.multiple_of(16 * gy, 16), 16), 128 * h : 128 * h + 128]
-    out = pltpu.make_async_copy(vout, vout_h, lsem.at[0])
-    out.start()
-    out_copies.append(out)
     for c in ice_in:
         c.wait_recv()
     for j in range(0, 2048, 512):
@@ -680,13 +676,8 @@
         scale = drag[:, s] * jnp.sqrt(a * a + b * b)
         stress[0, :, s] = scale * (COS * a - SIN * b)
         stress[1, :, s] = scale * (SIN * a + COS * b)
-    out = pltpu.make_async_copy(stress, stress_h, lsem.at[1])
-    out.start()
-    out_copies.append(out)
     for c in sent:
         c.wait_send()
-    for c in out_copies:
-        c.wait()
 
 
 def on_device(velocity, residual, east, north, coriolis, land, ocean_velocity, owner, tile_drag):
@@ -700,6 +691,7 @@
         return [vm(3, n, 128), vm(2, n, 128), vm(3, n, 128), vm(1, 2, n, 128), vm(1, 2, n, 128), vm(1, 2, n, 128)]
 
     scratch = [
+        pltpu.SMEM((OTILES,), f32),
         vm(2, 6, 304, 128), vm(304, 128, dtype=jnp.int32), vm(2, 256, 128), vm(2, 16, 2048),
         vm(16, 2048, dtype=jnp.int32), vm(16, 2048),
         vm(2, 2, 304, 128), vm(2, 2, 304, 128), vm(2, 304, 128), vm(2, 304, 128), vm(2, 304, 128),
@@ -710,23 +702,21 @@
         *level(144), *level(128), *level(64), *level(32),
         vm(16, 2, 8, 128), vm(2, 8, 128), vm(2, 64, 128), vm(16, 8, 128), vm(8, 128), vm(64, 128),
         vm(7, 80, 128), vm(2, 80, 128), vm(2, 80, 128),
-        vm(2, 2, 304, 128), vm(2, 24, 128), vm(2, 256, 128), vm(2, 128, 256), vm(2, 16, 2048), vm(2, 16, 2048),
-        pltpu.SemaphoreType.DMA((8,)),
+        vm(2, 2, 304, 128), vm(2, 24, 128), vm(2, 128, 256), vm(2, 16, 2048),
+        pltpu.SemaphoreType.DMA((9,)),
     ]
     for count in (10, 2, 4, 8, 8, 15, 7, 15, 7, 14):
         scratch += [pltpu.SemaphoreType.DMA((count,))] * 2
-    hbm = pl.BlockSpec(memory_space=pl.ANY)
+    hbm = pl.BlockSpec(memory_space=pltpu.HBM)
+    vmem = pl.BlockSpec(memory_space=pltpu.VMEM)
     return pl.pallas_call(
         kernel,
-        out_shape=(
-            jax.ShapeDtypeStruct((2, 256, 128), f32),
-            jax.ShapeDtypeStruct((2, 16, 2048), f32),
-        ),
-        in_specs=[hbm] * 8 + [pl.BlockSpec(memory_space=pltpu.SMEM)],
-        out_specs=(hbm, hbm),
+        out_shape=(pltpu.VMEM((2, 256, 128), f32), pltpu.VMEM((2, 16, 2048), f32)),
+        in_specs=[hbm] * 9,
+        out_specs=(vmem, vmem),
         scratch_shapes=scratch,
         compiler_params=pltpu.CompilerParams(
-            collective_id=0, has_side_effects=True, vmem_limit_bytes=48 * 1024 * 1024
+            collective_id=0, has_side_effects=True, vmem_limit_bytes=63 * 1024 * 1024
         ),
     )(velocity, residual, east, north, coriolis, land, ocean_velocity, owner, tile_drag)
 

time: 54.2 us -> 44.6 us (0.82)
  local copies, waits for them, and re-layouts: 9.42 us -> 1.41 us
  Pallas kernels: 43.8 us -> 42.4 us
    unnamed x20 -> x2, local copies, waits for them, and re-layouts: 9.42 us -> 1.41 us
    pallas_call x1, Pallas kernels: 43.8 us -> 42.4 us  [on_device(): pl.pallas_call(kernel, out_shape=(pltpu.VMEM((2, 256, 128), f32), pltpu.V...]
where the time goes in v2:
time: 44.6 us; the launch traced here: 44.4 us
  Pallas kernels  42.4 us (95%)
  local copies, waits for them, and re-layouts  1.41 us (3%)
  between operations  0.64 us (1%)
    pallas_call x1, Pallas kernels, on_device(): pl.pallas_call(kernel, out_shape=(pltpu.VMEM((2, 256, 128), f32), pltpu.V...  42.4 us
    unnamed x2, local copies, waits for them, and re-layouts  1.41 us

profile of v2, /device:TPU:1, one launch (start us, length us, event | category | flops | bytes accessed | tf_op | source)
XLA Modules:
  0.0 44.4 jit_solution(9512036666725086140)
XLA Ops:
  0.6 42.4 %shard_map.104 = (f32[2,256,128]{2,1,0:T(8,128)S(1)}, f32[2,16,2048]{2,1,0:T(8,128)S(1)}) custom-call(f32[2,256,128]{2,1,0:T(8,128)} %vel_h.1, f32[2,256,128]{2,1,0:T(8,128)} %res_h.1, f32[256,128]{1,0:T(8,128)} %east_h.1, f32[256,128]{1,0:T(8,128)} %north_h.1, f32[256,128]{1,0:T(8,128)} %cor_h.1, s32[256,128]{1,0:T(8,128)} %land_h.1, f32[2,16,2048]{2,1,0:T(8,128)} %ocv_h.1, ...), custom_call_target="tpu_custom_call" | custom-call | tf_op jit(solution)/shard_map/pallas_call | solution.py:712
  43.0 0.7 %copy.13 = f32[2,256,128]{2,1,0:T(8,128)} copy(f32[2,256,128]{2,1,0:T(8,128)S(1)} %get-tuple-element.2) | data formatting | bytes 524288
  43.7 0.7 %copy.14 = f32[2,16,2048]{2,1,0:T(8,128)} copy(f32[2,16,2048]{2,1,0:T(8,128)S(1)} %get-tuple-element.3) | data formatting | bytes 524288

commit v3 on v2

--- a/solution.py
+++ b/solution.py
@@ -1,3 +1,4 @@
+import functools
 import math
 
 import jax
@@ -21,7 +22,8 @@
 BASE = [0, 21, 42, 63, 84, 105]
 FIRST = [118, 118, 118, 118, 118, 117]
 TOP, OWN, BOT, END = 8, 24, 280, 296
-NEIGHBOURS = [(dx, dy) for dy in (-1, 0, 1) for dx in (-1, 0, 1) if (dx, dy) != (0, 0)]
+NEIGHBOURS = [(1, 1), (-1, 1), (1, -1), (-1, -1), (1, 0), (-1, 0), (0, 1), (0, -1)]
+FAR_FIRST = sorted(range(1, GX), key=lambda o: -min(o % 4, 4 - o % 4) - min(o // 4, 4 - o // 4))
 
 
 def lane_of(n):
@@ -169,25 +171,74 @@
     l2c, l2b, l2w, x2, y2, rr2,
     l3c, l3b, l3w, x3, y3, rr3,
     l4c, l4b, l4w, x4, y4, rr4,
-    g1c, s1c, c5, g1b, s1b, b5, w5, x5, y5,
+    g1c, s1c, c5, g1b, s1b, b5, b5f, w5, x5, y5, whole,
     up, up5, turned, ice,
     lsem, ns_s, ns_r, ew_s, ew_r, co_s, co_r, p2_s, p2_r, b2_s, b2_r,
-    c1_s, c1_r, c2_s, c2_r, b1_s, b1_r, bb_s, bb_r, at_s, at_r,
+    c1_s, c1_r, c2_s, c2_r, b1_s, b1_r, bb_s, bb_r, at_s, at_r, known,
 ):
     gx, gy = lax.axis_index("gx"), lax.axis_index("gy")
 
     def at(dx, dy):
         return (lax.rem(gx + dx + GX, GX), lax.rem(gy + dy + GY, GY))
 
+    def inside(dx, dy):
+        tests = [gx + dx < GX] * (dx > 0) + [gx + dx >= 0] * (dx < 0)
+        tests += [gy + dy < GY] * (dy > 0) + [gy + dy >= 0] * (dy < 0)
+        return functools.reduce(jnp.logical_and, tests)
+
+    def one_if(dx, dy):
+        return jnp.where(inside(dx, dy), 1, 0)
+
+    def signal(sem, dx, dy):
+        @pl.when(inside(dx, dy))
+        def _():
+            pl.semaphore_signal(sem, inc=1, device_id=at(dx, dy), device_id_type=MESH)
+
+    barrier = pltpu.get_barrier_semaphore()
+    for dx, dy in NEIGHBOURS:
+        signal(barrier, dx, dy)
+
+    def greet(step):
+        for k, (dx, dy) in enumerate(((1, 0), (0, 1))):
+            if step < 4 - k:
+                for sign in (1, -1):
+                    signal(known.at[2 * step + k], sign * dx << step, sign * dy << step)
+
+    def greeted(step):
+        for k, (dx, dy) in enumerate(((1, 0), (0, 1))):
+            if step < 4 - k:
+                dx, dy = dx << step, dy << step
+                pl.semaphore_wait(known.at[2 * step + k], one_if(dx, dy) + one_if(-dx, -dy))
+
     sent = []
 
-    def send(src, dst, s, r, dev):
-        c = pltpu.make_async_remote_copy(
-            src_ref=src, dst_ref=dst, send_sem=s, recv_sem=r, device_id=dev, device_id_type=MESH
-        )
-        c.start()
-        sent.append(c)
-        return c
+    class Message:
+        def __init__(self, src, dst, s, r, dx, dy, whole=False):
+            self.make = lambda: pltpu.make_async_remote_copy(
+                src_ref=src, dst_ref=dst, send_sem=s, recv_sem=r, device_id=at(dx, dy), device_id_type=MESH
+            )
+            self.to = None if whole else inside(dx, dy)
+            self.come = None if whole else inside(-dx, -dy)
+            self.run(self.to, lambda c: c.start())
+            sent.append(self)
+
+        def run(self, cond, act):
+            if cond is None:
+                act(self.make())
+            else:
+                pl.when(cond)(lambda: act(self.make()))
+
+        def wait_recv(self):
+            self.run(self.come, lambda c: c.wait_recv())
+
+        def wait_send(self):
+            self.run(self.to, lambda c: c.wait_send())
+
+    def send(src, dst, s, r, to):
+        return Message(src, dst, s, r, *to)
+
+    def send_all(src, dst, s, r, dx, dy):
+        return Message(src, dst, s, r, dx, dy, True)
 
     def load(src, dst, k):
         c = pltpu.make_async_copy(src, dst, lsem.at[k])
@@ -202,12 +253,6 @@
         load(land_h, land.at[OWN:BOT, :], 4),
     ]
     late = [load(own_h, owner, 5), load(ocv_h, ocv, 6), load(vel_h, vel, 7), load(drag_h, drag_s, 8)]
-
-    barrier = pltpu.get_barrier_semaphore()
-    met = [at(dx, dy) for dx, dy in NEIGHBOURS]
-    met += [at(o, 0) for o in range(2, GX - 1)] + [at(0, o) for o in range(2, GY - 1)]
-    for dev in met:
-        pl.semaphore_signal(barrier, inc=1, device_id=dev, device_id_type=MESH)
 
     zero = jnp.zeros((8, 128), jnp.float32)
     for t in range(2):
@@ -222,12 +267,79 @@
             for c in range(2):
                 ref[0, c, 0:8, :] = zero
                 ref[0, c, 8 + rows : 16 + rows, :] = zero
-    for ref in (x5, y5):
-        for c in range(2):
-            ref[c, 0:8, :] = zero
-            ref[c, 72:80, :] = zero
-
-    pl.semaphore_wait(barrier, len(met))
+    blank = jnp.zeros((128, 128), jnp.float32)
+    for cond, side, k in ((gx == 0, got_l, 0), (gx == GX - 1, got_r, 2)):
+
+        @pl.when(cond)
+        def _(side=side, k=k):
+            side[...] = blank
+            g2[k] = blank
+            for dy in range(3):
+                gb2[dy, k] = blank[0:32]
+            for q in range(2):
+                corner[2 * q + k // 2] = blank[0:16]
+
+    for cond, r, k, q in ((gy == 0, TOP, 0, 0), (gy == GY - 1, BOT, 2, 2)):
+
+        @pl.when(cond)
+        def _(r=r, k=k, q=q):
+            for p in (B0, B1, FF, NN, EE):
+                p0[0, p, r : r + 16, :] = blank[0:16]
+            land[r : r + 16, :] = jnp.zeros((16, 128), jnp.int32)
+            for c in range(3):
+                g2[c, 48 * k : 48 * k + 32, :] = blank[0:32]
+                gb2[k, c] = blank[0:32]
+            for c in range(2):
+                corner[q + c] = blank[0:16]
+
+    whole[0:8, :] = zero
+    whole[72:80, :] = zero
+
+    for c in loads:
+        c.wait()
+
+    def is_right(n):
+        lane = lane_of(n)
+        out = within(lane, 105, 116)
+        for p in range(5):
+            out = jnp.logical_or(out, within(lane, BASE[p], BASE[p] + 10))
+        return out
+
+    def is_left(n):
+        lane = lane_of(n)
+        out = within(lane, 116, 126)
+        for p in range(5):
+            out = jnp.logical_or(out, within(lane, BASE[p] + 10, BASE[p] + 20))
+        return out
+
+    for r in range(0, 256, 32):
+        lane = lane_of(32)
+        p0[0, OC, OWN + r : OWN + r + 32, :] = (1 - land[OWN + r : OWN + r + 32, :]).astype(jnp.float32)
+        packed = roll(p0[0, EE, OWN + r : OWN + r + 32, :], BASE[EE] - FIRST[EE])
+        for p in (NN, OC, FF, B1, B0):
+            part = roll(p0[0, p, OWN + r : OWN + r + 32, :], BASE[p] - FIRST[p])
+            packed = jnp.where(lane < BASE[p] + 21, part, packed)
+        cbuf[r : r + 32, :] = packed
+    for r in range(0, 128, 32):
+        a, b = cbuf[r : r + 32, :], cbuf[128 + r : 160 + r, :]
+        mr[r : r + 32, :] = jnp.where(is_right(32), a, roll(b, 11))
+        ml[r : r + 32, :] = jnp.where(is_left(32), a, roll(b, -11))
+    pl.semaphore_wait(barrier, functools.reduce(jnp.add, [one_if(*d) for d in NEIGHBOURS]))
+    edge_in = [
+        send(cbuf.at[240:256, :], corner.at[0], co_s.at[0], co_r.at[0], (1, 1)),
+        send(cbuf.at[240:256, :], corner.at[1], co_s.at[1], co_r.at[1], (-1, 1)),
+        send(cbuf.at[0:16, :], corner.at[2], co_s.at[2], co_r.at[2], (1, -1)),
+        send(cbuf.at[0:16, :], corner.at[3], co_s.at[3], co_r.at[3], (-1, -1)),
+    ]
+    side_in = []
+    for k in range(4):
+        part = pl.ds(32 * k, 32)
+        side_in.append(
+            [
+                send(mr.at[part, :], got_l.at[part, :], ew_s.at[2 * k], ew_r.at[2 * k], (1, 0)),
+                send(ml.at[part, :], got_r.at[part, :], ew_s.at[2 * k + 1], ew_r.at[2 * k + 1], (-1, 0)),
+            ]
+        )
 
     rows_in = []
     for k, (src, dst) in enumerate(
@@ -241,46 +353,9 @@
     ):
         last = src.at[:, 240:256, :] if k == 0 else src.at[240:256, :]
         first = src.at[:, 0:16, :] if k == 0 else src.at[0:16, :]
-        rows_in.append(send(last, dst(TOP, OWN), ns_s.at[2 * k], ns_r.at[2 * k], at(0, 1)))
-        rows_in.append(send(first, dst(BOT, END), ns_s.at[2 * k + 1], ns_r.at[2 * k + 1], at(0, -1)))
-
-    for c in loads:
-        c.wait()
-
-    def is_right(n):
-        lane = lane_of(n)
-        out = within(lane, 105, 116)
-        for p in range(5):
-            out = jnp.logical_or(out, within(lane, BASE[p], BASE[p] + 10))
-        return out
-
-    def is_left(n):
-        lane = lane_of(n)
-        out = within(lane, 116, 126)
-        for p in range(5):
-            out = jnp.logical_or(out, within(lane, BASE[p] + 10, BASE[p] + 20))
-        return out
-
-    for r in range(0, 256, 32):
-        lane = lane_of(32)
-        p0[0, OC, OWN + r : OWN + r + 32, :] = (1 - land[OWN + r : OWN + r + 32, :]).astype(jnp.float32)
-        packed = roll(p0[0, EE, OWN + r : OWN + r + 32, :], BASE[EE] - FIRST[EE])
-        for p in (NN, OC, FF, B1, B0):
-            part = roll(p0[0, p, OWN + r : OWN + r + 32, :], BASE[p] - FIRST[p])
-            packed = jnp.where(lane < BASE[p] + 21, part, packed)
-        cbuf[r : r + 32, :] = packed
-    for r in range(0, 128, 32):
-        a, b = cbuf[r : r + 32, :], cbuf[128 + r : 160 + r, :]
-        mr[r : r + 32, :] = jnp.where(is_right(32), a, roll(b, 11))
-        ml[r : r + 32, :] = jnp.where(is_left(32), a, roll(b, -11))
-    edge_in = [
-        send(mr, got_l, ew_s.at[0], ew_r.at[0], at(1, 0)),
-        send(ml, got_r, ew_s.at[1], ew_r.at[1], at(-1, 0)),
-        send(cbuf.at[240:256, :], corner.at[0], co_s.at[0], co_r.at[0], at(1, 1)),
-        send(cbuf.at[240:256, :], corner.at[1], co_s.at[1], co_r.at[1], at(-1, 1)),
-        send(cbuf.at[0:16, :], corner.at[2], co_s.at[2], co_r.at[2], at(1, -1)),
-        send(cbuf.at[0:16, :], corner.at[3], co_s.at[3], co_r.at[3], at(-1, -1)),
-    ]
+        rows_in.append(send(last, dst(TOP, OWN), ns_s.at[2 * k], ns_r.at[2 * k], (0, 1)))
+        rows_in.append(send(first, dst(BOT, END), ns_s.at[2 * k + 1], ns_r.at[2 * k + 1], (0, -1)))
+    greet(0)
 
     def thinned(load_e, load_n, load_f, n):
         e = (load_e(0) + load_e(1)) * 0.25
@@ -313,7 +388,7 @@
             src, dst = p2.at[32:64, :], g2.at[1 - dx, 0:32, :]
         else:
             src, dst = p2.at[0:32, :], g2.at[1 - dx, 96:128, :]
-        coef_in.append(send(src, dst, p2_s.at[k], p2_r.at[k], at(dx, dy)))
+        coef_in.append(send(src, dst, p2_s.at[k], p2_r.at[k], (dx, dy)))
     g2[1, 32:96, :] = p2[...]
 
     lane = lane_of(8)
@@ -324,9 +399,6 @@
     e5, n5, f5 = (take(oc5[p], idx5) for p in range(3))
     g1c[0, 0] = jnp.where(here0, e5, jnp.where(here1, n5, 0.0))
     g1c[0, 1] = jnp.where(here0, f5, 0.0)
-    gat_c = [
-        send(g1c.at[0], g1c.at[o], c1_s.at[o - 1], c1_r.at[o - 1], at(o, 0)) for o in range(1, GX)
-    ]
 
     for c in late:
         c.wait()
@@ -338,29 +410,43 @@
             dr = jnp.where(ow == k, tiles[k], dr)
         drag[:, j : j + 512] = dr
 
-    for c in rows_in + edge_in:
-        c.wait_recv()
-
-    def spread(packed, r):
-        lane, row = lane_of(16), row_of(16) + (r - OWN)
-        col = jnp.where(lane < 64, lane + 128, lane - 128) + 128 * gx
-        inside = jnp.logical_and(within(col, 0, 128 * GX), within(row + 256 * gy, 0, 256 * GY))
-        near = jnp.logical_or(lane < 10, lane >= 118)
+    greeted(0)
+    greet(1)
+    greeted(1)
+    greet(2)
+
+    lane = lane_of(16)
+    col = jnp.where(lane < 64, lane + 128, lane - 128) + 128 * gx
+    beside = within(col, 0, 128 * GX)
+    near = jnp.logical_and(beside, jnp.logical_or(lane < 10, lane >= 118))
+    right = is_right(16)
+
+    def spread(packed, r, beside, near):
         for p in range(6):
             v = roll(packed, FIRST[p] - BASE[p])
             if p == OC:
-                v = jnp.where(jnp.logical_and(inside, near), v, 0.0)
+                v = jnp.where(near, v, 0.0)
             elif p in (NN, EE):
-                v = jnp.where(inside, v, 0.0)
+                v = jnp.where(beside, v, 0.0)
             p0[1, p, r : r + 16, :] = v
 
-    right = is_right(16)
-    for r in range(0, 128, 16):
-        a, b = got_l[r : r + 16, :], got_r[r : r + 16, :]
-        spread(jnp.where(right, a, b), OWN + r)
-        spread(jnp.where(right, roll(a, -11), roll(b, 11)), OWN + 128 + r)
-    spread(jnp.where(right, corner[0], corner[1]), TOP)
-    spread(jnp.where(right, corner[2], corner[3]), BOT)
+    for k in range(4):
+        for c in side_in[k]:
+            c.wait_recv()
+        for r in range(32 * k, 32 * k + 32, 16):
+            a, b = got_l[r : r + 16, :], got_r[r : r + 16, :]
+            spread(jnp.where(right, a, b), OWN + r, beside, near)
+            spread(jnp.where(right, roll(a, -11), roll(b, 11)), OWN + 128 + r, beside, near)
+    for c in rows_in + edge_in:
+        c.wait_recv()
+    greeted(2)
+    greet(3)
+    for k, r, there in ((0, TOP, gy > 0), (2, BOT, gy < GY - 1)):
+        keep = jnp.where(there, 1, 0)
+        spread(
+            jnp.where(right, corner[k], corner[k + 1]), r,
+            jnp.logical_and(beside, row_of(16) < 16 * keep), jnp.logical_and(near, row_of(16) < 16 * keep),
+        )
     for r, there in ((TOP, gy > 0), (BOT, gy < GY - 1)):
         keep = jnp.where(there, 1.0, 0.0)
         p0[0, OC, r : r + 16, :] = (1 - land[r : r + 16, :]).astype(jnp.float32) * keep
@@ -444,8 +530,12 @@
     )
     res_in = []
     for k, (dx, dy) in enumerate(NEIGHBOURS):
-        res_in.append(send(m2, gb2.at[1 - dy, 1 - dx], b2_s.at[k], b2_r.at[k], at(dx, dy)))
-
+        res_in.append(send(m2, gb2.at[1 - dy, 1 - dx], b2_s.at[k], b2_r.at[k], (dx, dy)))
+
+    greeted(3)
+    gat_c = [
+        send_all(g1c.at[0], g1c.at[o], c1_s.at[o - 1], c1_r.at[o - 1], o, 0) for o in FAR_FIRST
+    ]
     for c in coef_in:
         c.wait_recv()
     for r in range(0, 128, 32):
@@ -493,21 +583,11 @@
         for r, n in lev.chunks():
             lev.setup(masks[lev], r, n)
 
-    for c in gat_c:
-        c.wait_recv()
-
     def total(g):
         parts = [g[k] for k in range(GX)]
         while len(parts) > 1:
             parts = [parts[i] + parts[i + 1] for i in range(0, len(parts), 2)]
         return parts[0]
-
-    mine = pl.ds(pl.multiple_of(8 * gy, 8), 8)
-    s1c[...] = total(g1c)
-    c5[:, mine, :] = s1c[...]
-    gat_c2 = [
-        send(s1c, c5.at[:, mine, :], c2_s.at[o - 1], c2_r.at[o - 1], at(0, o)) for o in range(1, GY)
-    ]
 
     for c in res_in:
         c.wait_recv()
@@ -543,64 +623,80 @@
         u.append(take((v + roll(v, -4)) * 0.25, 8 * idx5))
     g1b[0] = jnp.where(here0, u[0], jnp.where(here1, u[1], 0.0))
     gat_b = [
-        send(g1b.at[0], g1b.at[o], b1_s.at[o - 1], b1_r.at[o - 1], at(o, 0)) for o in range(1, GX)
+        send_all(g1b.at[0], g1b.at[o], b1_s.at[o - 1], b1_r.at[o - 1], o, 0) for o in FAR_FIRST
+    ]
+    for c in gat_c:
+        c.wait_recv()
+    mine = pl.ds(pl.multiple_of(8 * gy, 8), 8)
+    s1c[...] = total(g1c)
+    c5[:, mine, :] = s1c[...]
+    gat_c2 = [
+        send_all(s1c, c5.at[:, mine, :], c2_s.at[o - 1], c2_r.at[o - 1], 0, o) for o in (4, 3, 5, 2, 6, 1, 7)
     ]
     for c in gat_c2:
         c.wait_recv()
-    n = 64
-    lane, row = lane_of(n), row_of(n)
+    lane = lane_of(32)
     first = lane < 64
 
-    def both(v):
-        return jnp.where(first, v, roll(v, 64))
-
-    en = c5[0]
-    e5, n5, f5 = both(en), both(roll(en, 64)), both(c5[1])
+    def folded(v, half):
+        a, b = v[0:32], v[32:64]
+        if half:
+            return jnp.where(first, roll(a, 64), b)
+        return jnp.where(first, a, roll(b, 64))
+
+    e5, n5, f5 = folded(c5[0], 0), folded(c5[0], 1), folded(c5[1], 0)
     col = lane & 63
     ecut = jnp.where(col == 63, 0.0, e5)
     wcut = jnp.where(col == 0, 0.0, roll(e5, 1))
-    w5[0, 0:8, :] = zero
-    w5[0, 8:72, :] = n5
-    s5 = w5[0, 7:71, :]
+    w5[0, 8:40, :] = n5
+    w5[0, 0:8, :] = jnp.where(lane_of(8) < 64, 0.0, roll(n5[24:32], 64))
+    s5 = w5[0, 7:39, :]
     diag = MASS + e5 + wcut + n5 + s5
     g = RELAX / (diag * diag + f5 * f5)
-    pd5 = g * diag
-    pf5 = jnp.where(first, g * f5, -(g * f5))
+    w5[1, 8:40, :] = ecut
+    w5[2, 8:40, :] = wcut
+    w5[3, 8:40, :] = s5
+    w5[4, 8:40, :] = g * diag
+    w5[5, 8:40, :] = g * f5
+    w5[0, 8:40, :] = jnp.where(jnp.logical_and(row_of(32) == 31, lane >= 64), 0.0, n5)
 
     for c in gat_b:
         c.wait_recv()
     s1b[...] = total(g1b)
     b5[mine, :] = s1b[...]
     gat_b2 = [
-        send(s1b, b5.at[mine, :], bb_s.at[o - 1], bb_r.at[o - 1], at(0, o)) for o in range(1, GY)
+        send_all(s1b, b5.at[mine, :], bb_s.at[o - 1], bb_r.at[o - 1], 0, o) for o in (4, 3, 5, 2, 6, 1, 7)
     ]
-    w5[1, 8:72, :] = ecut
-    w5[2, 8:72, :] = wcut
-    w5[3, 8:72, :] = s5
-    w5[4, 8:72, :] = pd5
-    w5[5, 8:72, :] = pf5
     for c in gat_b2:
         c.wait_recv()
+
+    def put(ref, c, v):
+        ref[c, 8:40, :] = v
+        ref[c, 40:48, :] = roll(v[0:8], 64)
+        ref[c, 0:8, :] = roll(v[24:32], 64)
+
     rhs = b5[...]
-    other = roll(rhs, 64)
-    x5[0, 8:72, :] = w5[4, 8:72, :] * rhs + w5[5, 8:72, :] * other
-    x5[1, 8:72, :] = w5[4, 8:72, :] * other - w5[5, 8:72, :] * rhs
-    w5[6, 8:72, :] = other
+    b5f[0] = folded(rhs, 0)
+    b5f[1] = folded(rhs, 1)
+    put(x5, 0, w5[4, 8:40, :] * b5f[0] + w5[5, 8:40, :] * b5f[1])
+    put(x5, 1, w5[4, 8:40, :] * b5f[1] - w5[5, 8:40, :] * b5f[0])
     here, there = x5, y5
     for _ in range(SWEEPS - 1):
         t = []
         for c in range(2):
-            x = here[c, 8:72, :]
+            x = here[c, 8:40, :]
             t.append(
-                ((b5[...] if c == 0 else w5[6, 8:72, :]) + w5[1, 8:72, :] * roll(x, -1))
-                + (w5[2, 8:72, :] * roll(x, 1) + w5[0, 8:72, :] * here[c, 9:73, :])
-                + w5[3, 8:72, :] * here[c, 7:71, :]
+                (b5f[c] + w5[0, 8:40, :] * here[c, 9:41, :])
+                + w5[3, 8:40, :] * here[c, 7:39, :]
+                + (w5[1, 8:40, :] * roll(x, -1) + w5[2, 8:40, :] * roll(x, 1))
             )
-        there[0, 8:72, :] = KEEP * here[0, 8:72, :] + w5[4, 8:72, :] * t[0] + w5[5, 8:72, :] * t[1]
-        there[1, 8:72, :] = KEEP * here[1, 8:72, :] + w5[4, 8:72, :] * t[1] - w5[5, 8:72, :] * t[0]
+        put(there, 0, KEEP * here[0, 8:40, :] + w5[4, 8:40, :] * t[0] + w5[5, 8:40, :] * t[1])
+        put(there, 1, KEEP * here[1, 8:40, :] + w5[4, 8:40, :] * t[1] - w5[5, 8:40, :] * t[0])
         here, there = there, here
-
-    near = here[0, pl.ds(pl.multiple_of(8 * gy, 8), 24), :]
+    whole[8:40, :] = jnp.where(first, here[0, 8:40, :], roll(here[1, 8:40, :], 64))
+    whole[40:72, :] = jnp.where(first, roll(here[0, 8:40, :], 64), here[1, 8:40, :])
+
+    near = whole[pl.ds(pl.multiple_of(8 * gy, 8), 24), :]
     lane = lane_of(24)
     col = 4 * gx + (jnp.where(lane < 64, lane, lane - 128) >> 3)
     idx = jnp.clip(col, 0, 63)
@@ -641,15 +737,22 @@
                 w = take(v, idx + 64 * t)
                 up[t, c, pl.ds(8 + 2 * r, 48, 2), :] = w
                 up[t, c, pl.ds(9 + 2 * r, 48, 2), :] = w
-    for r, n in fine.chunks():
-        for t in range(2):
-            m = ocean(t, r, n)
-            for c in range(2):
-                y0[t, c, pl.ds(r, n), :] = y0[t, c, pl.ds(r, n), :] + m * up[t, c, pl.ds(r, n), :]
-    fine.sweep(y0, x0, 16, 288)
-
-    ice_in = []
+    def corrected(lo, hi):
+        for r, n in fine.chunks(lo, hi):
+            for t in range(2):
+                m = ocean(t, r, n)
+                for c in range(2):
+                    y0[t, c, pl.ds(r, n), :] = y0[t, c, pl.ds(r, n), :] + m * up[t, c, pl.ds(r, n), :]
+
+    corrected(8, 168)
+    fine.sweep(y0, x0, 16, 160)
+
+    ice_in = {}
+    before = list(sent)
     for h in range(2):
+        if h == 1:
+            corrected(168, 296)
+            fine.sweep(y0, x0, 160, 288)
         for r in range(128 * h, 128 * h + 128, 32):
             new = fine.relaxed(x0, OWN + r, 32, 1)[0]
             for c in range(2):
@@ -657,26 +760,28 @@
         for c in range(2):
             turned[c, :, 128 * h : 128 * h + 128] = vout[c, 128 * h : 128 * h + 128, :].T
         lanes = pl.ds(pl.multiple_of(256 * gy + 128 * h, 128), 128)
-        for o in range(1, GY):
+        for o in (4, 3, 5, 2, 6, 1, 7):
             dev = at(0, o)
             k = 7 * h + o - 1
-            ice_in.append(
-                send(
-                    turned.at[:, pl.ds(pl.multiple_of(16 * dev[1], 16), 16), 128 * h : 128 * h + 128],
-                    ice.at[:, :, lanes],
-                    at_s.at[k], at_r.at[k], dev,
-                )
+            ice_in[o, h] = send_all(
+                turned.at[:, pl.ds(pl.multiple_of(16 * dev[1], 16), 16), 128 * h : 128 * h + 128],
+                ice.at[:, :, lanes],
+                at_s.at[k], at_r.at[k], 0, o,
             )
-        ice[:, :, lanes] = turned[:, pl.ds(pl.multiple_of(16 * gy, 16), 16), 128 * h : 128 * h + 128]
-    for c in ice_in:
-        c.wait_recv()
-    for j in range(0, 2048, 512):
-        s = slice(j, j + 512)
+    mine = pl.ds(pl.multiple_of(16 * gy, 16), 16)
+    ice[:, :, pl.ds(pl.multiple_of(256 * gy, 256), 256)] = turned[:, mine, :]
+    for c in before:
+        c.wait_send()
+    for o in (0, 1, 7, 2, 6, 3, 5, 4):
+        if o:
+            ice_in[o, 0].wait_recv()
+            ice_in[o, 1].wait_recv()
+        s = pl.ds(pl.multiple_of(256 * at(0, -o)[1], 256), 256)
         a, b = ice[0, :, s] - ocv[0, :, s], ice[1, :, s] - ocv[1, :, s]
         scale = drag[:, s] * jnp.sqrt(a * a + b * b)
         stress[0, :, s] = scale * (COS * a - SIN * b)
         stress[1, :, s] = scale * (SIN * a + COS * b)
-    for c in sent:
+    for c in ice_in.values():
         c.wait_send()
 
 
@@ -701,12 +806,13 @@
         vm(64, 128), vm(3, 128, 128), vm(32, 128), vm(3, 3, 32, 128),
         *level(144), *level(128), *level(64), *level(32),
         vm(16, 2, 8, 128), vm(2, 8, 128), vm(2, 64, 128), vm(16, 8, 128), vm(8, 128), vm(64, 128),
-        vm(7, 80, 128), vm(2, 80, 128), vm(2, 80, 128),
+        vm(2, 32, 128), vm(6, 48, 128), vm(2, 48, 128), vm(2, 48, 128), vm(80, 128),
         vm(2, 2, 304, 128), vm(2, 24, 128), vm(2, 128, 256), vm(2, 16, 2048),
         pltpu.SemaphoreType.DMA((9,)),
     ]
-    for count in (10, 2, 4, 8, 8, 15, 7, 15, 7, 14):
+    for count in (10, 8, 4, 8, 8, 15, 7, 15, 7, 14):
         scratch += [pltpu.SemaphoreType.DMA((count,))] * 2
+    scratch.append(pltpu.SemaphoreType.REGULAR((8,)))
     hbm = pl.BlockSpec(memory_space=pltpu.HBM)
     vmem = pl.BlockSpec(memory_space=pltpu.VMEM)
     return pl.pallas_call(

time: 44.6 us -> 41.4 us (0.928)
  Pallas kernels: 42.4 us -> 39.3 us
    pallas_call x1, Pallas kernels: 42.4 us -> 39.3 us  [on_device(): pl.pallas_call(kernel, out_shape=(pltpu.VMEM((2, 256, 128), f32), pltpu.V...]
where the time goes in v3:
time: 41.4 us; the launch traced here: 41.3 us
  Pallas kernels  39.3 us (95%)
  local copies, waits for them, and re-layouts  1.41 us (3%)
  between operations  0.64 us (2%)
    pallas_call x1, Pallas kernels, on_device(): pl.pallas_call(kernel, out_shape=(pltpu.VMEM((2, 256, 128), f32), pltpu.V...  39.3 us
    unnamed x2, local copies, waits for them, and re-layouts  1.41 us

profile of v3, /device:TPU:1, one launch (start us, length us, event | category | flops | bytes accessed | tf_op | source)
XLA Modules:
  0.0 41.3 jit_solution(13165705335306390417)
XLA Ops:
  0.6 39.3 %shard_map.104 = (f32[2,256,128]{2,1,0:T(8,128)S(1)}, f32[2,16,2048]{2,1,0:T(8,128)S(1)}) custom-call(f32[2,256,128]{2,1,0:T(8,128)} %vel_h.1, f32[2,256,128]{2,1,0:T(8,128)} %res_h.1, f32[256,128]{1,0:T(8,128)} %east_h.1, f32[256,128]{1,0:T(8,128)} %north_h.1, f32[256,128]{1,0:T(8,128)} %cor_h.1, s32[256,128]{1,0:T(8,128)} %land_h.1, f32[2,16,2048]{2,1,0:T(8,128)} %ocv_h.1, ...), custom_call_target="tpu_custom_call" | custom-call | tf_op jit(solution)/shard_map/pallas_call | solution.py:818
  39.9 0.7 %copy.13 = f32[2,256,128]{2,1,0:T(8,128)} copy(f32[2,256,128]{2,1,0:T(8,128)S(1)} %get-tuple-element.2) | data formatting | bytes 524288
  40.6 0.7 %copy.14 = f32[2,16,2048]{2,1,0:T(8,128)} copy(f32[2,16,2048]{2,1,0:T(8,128)S(1)} %get-tuple-element.3) | data formatting | bytes 524288

commit v4 on v3

--- a/solution.py
+++ b/solution.py
@@ -439,8 +439,6 @@
             spread(jnp.where(right, roll(a, -11), roll(b, 11)), OWN + 128 + r, beside, near)
     for c in rows_in + edge_in:
         c.wait_recv()
-    greeted(2)
-    greet(3)
     for k, r, there in ((0, TOP, gy > 0), (2, BOT, gy < GY - 1)):
         keep = jnp.where(there, 1, 0)
         spread(
@@ -468,6 +466,8 @@
         fine.start(r, n, fine.setup(lambda t, r, n: ocean(t, r, n) > 0.5, r, n))
     fine.sweep(x0, y0)
     fine.residual(y0, ocean)
+    greeted(2)
+    greet(3)
 
     def single(lc, lb, lw, x, y, rr, rows, shift, chunk):
         return Level(
@@ -480,6 +480,21 @@
         )
 
     one = single(l1c, l1b, l1w, x1, y1, rr1, 144, 1, 48)
+    for r, n in ((0, 8), (8, 64), (72, 64), (136, 8)):
+        idx = (2 * lane_of(n)) & 127
+        low = lane_of(n) < 64
+
+        def part(t):
+            return thinned(
+                *(lambda odd, p=p: p0[t, p, pl.ds(TOP + 2 * r + odd, n, 2), :] for p in (EE, NN, FF)), n
+            )
+
+        far = part(1)
+        mid = part(0) if n == 8 else None
+        for p in range(3):
+            odd = 1 if p == 0 else 0
+            own = take(mid[p], idx + odd) if n == 8 else oc1[p, r - 8 : r - 8 + n, :]
+            l1c[p, 8 + r : 8 + r + n, :] = jnp.where(low, own, take(far[p], idx + odd))
     for r in range(0, 144, 48):
         n = 48
         idx = (2 * lane_of(n)) & 127
@@ -488,14 +503,6 @@
         def pick(pair, odd):
             return jnp.where(low, take(pair[0], idx + odd), take(pair[1], idx + odd))
 
-        parts = [
-            thinned(
-                *(lambda odd, p=p, t=t: p0[t, p, pl.ds(TOP + 2 * r + odd, n, 2), :] for p in (EE, NN, FF)), n
-            )
-            for t in range(2)
-        ]
-        for p in range(3):
-            l1c[p, 8 + r : 8 + r + n, :] = pick([parts[0][p], parts[1][p]], 1 if p == 0 else 0)
         for c in range(2):
             pair = []
             for t in range(2):
@@ -633,6 +640,13 @@
     gat_c2 = [
         send_all(s1c, c5.at[:, mine, :], c2_s.at[o - 1], c2_r.at[o - 1], 0, o) for o in (4, 3, 5, 2, 6, 1, 7)
     ]
+    for c in gat_b:
+        c.wait_recv()
+    s1b[...] = total(g1b)
+    b5[mine, :] = s1b[...]
+    gat_b2 = [
+        send_all(s1b, b5.at[mine, :], bb_s.at[o - 1], bb_r.at[o - 1], 0, o) for o in (4, 3, 5, 2, 6, 1, 7)
+    ]
     for c in gat_c2:
         c.wait_recv()
     lane = lane_of(32)
@@ -660,13 +674,6 @@
     w5[5, 8:40, :] = g * f5
     w5[0, 8:40, :] = jnp.where(jnp.logical_and(row_of(32) == 31, lane >= 64), 0.0, n5)
 
-    for c in gat_b:
-        c.wait_recv()
-    s1b[...] = total(g1b)
-    b5[mine, :] = s1b[...]
-    gat_b2 = [
-        send_all(s1b, b5.at[mine, :], bb_s.at[o - 1], bb_r.at[o - 1], 0, o) for o in (4, 3, 5, 2, 6, 1, 7)
-    ]
     for c in gat_b2:
         c.wait_recv()
 
@@ -678,23 +685,22 @@
     rhs = b5[...]
     b5f[0] = folded(rhs, 0)
     b5f[1] = folded(rhs, 1)
-    put(x5, 0, w5[4, 8:40, :] * b5f[0] + w5[5, 8:40, :] * b5f[1])
-    put(x5, 1, w5[4, 8:40, :] * b5f[1] - w5[5, 8:40, :] * b5f[0])
+    x = [w5[4, 8:40, :] * b5f[0] + w5[5, 8:40, :] * b5f[1], w5[4, 8:40, :] * b5f[1] - w5[5, 8:40, :] * b5f[0]]
     here, there = x5, y5
     for _ in range(SWEEPS - 1):
         t = []
         for c in range(2):
-            x = here[c, 8:40, :]
+            put(here, c, x[c])
+        for c in range(2):
             t.append(
-                (b5f[c] + w5[0, 8:40, :] * here[c, 9:41, :])
-                + w5[3, 8:40, :] * here[c, 7:39, :]
-                + (w5[1, 8:40, :] * roll(x, -1) + w5[2, 8:40, :] * roll(x, 1))
+                (b5f[c] + (w5[1, 8:40, :] * roll(x[c], -1) + w5[2, 8:40, :] * roll(x[c], 1)))
+                + (w5[0, 8:40, :] * here[c, 9:41, :] + w5[3, 8:40, :] * here[c, 7:39, :])
             )
-        put(there, 0, KEEP * here[0, 8:40, :] + w5[4, 8:40, :] * t[0] + w5[5, 8:40, :] * t[1])
-        put(there, 1, KEEP * here[1, 8:40, :] + w5[4, 8:40, :] * t[1] - w5[5, 8:40, :] * t[0])
+        pd, pf = w5[4, 8:40, :], w5[5, 8:40, :]
+        x = [KEEP * x[0] + (pd * t[0] + pf * t[1]), KEEP * x[1] + (pd * t[1] - pf * t[0])]
         here, there = there, here
-    whole[8:40, :] = jnp.where(first, here[0, 8:40, :], roll(here[1, 8:40, :], 64))
-    whole[40:72, :] = jnp.where(first, roll(here[0, 8:40, :], 64), here[1, 8:40, :])
+    whole[8:40, :] = jnp.where(first, x[0], roll(x[1], 64))
+    whole[40:72, :] = jnp.where(first, roll(x[0], 64), x[1])
 
     near = whole[pl.ds(pl.multiple_of(8 * gy, 8), 24), :]
     lane = lane_of(24)
@@ -710,14 +716,19 @@
     four.sweep(y4, x4)
     four.sweep(x4, y4)
 
-    for lev, coarse, rows in ((three, y4, 64), (two, y3, 128)):
-        for c in range(2):
-            v = coarse[0, c, 8 : 8 + rows // 2, :]
-            up[0, c, pl.ds(8, rows // 2, 2), :] = v
-            up[0, c, pl.ds(9, rows // 2, 2), :] = v
-            lev.y[0, c, 8 : 8 + rows, :] = lev.y[0, c, 8 : 8 + rows, :] + up[0, c, 8 : 8 + rows, :]
-        lev.sweep(lev.y, lev.x)
-        lev.sweep(lev.x, lev.y)
+    for lev, coarse, lo, hi, at_row, first_row, last_row in (
+        (three, y4, 8, 40, 8, 16, 64),
+        (two, y3, 16, 64, 24, 32, 112),
+    ):
+        n = hi - lo
+        for c in range(2):
+            v = coarse[0, c, lo:hi, :]
+            up[0, c, pl.ds(at_row, n, 2), :] = v
+            up[0, c, pl.ds(at_row + 1, n, 2), :] = v
+            rows = slice(at_row, at_row + 2 * n)
+            lev.y[0, c, rows, :] = lev.y[0, c, rows, :] + up[0, c, rows, :]
+        lev.sweep(lev.y, lev.x, first_row, last_row)
+        lev.sweep(lev.x, lev.y, first_row, last_row)
 
     lane = lane_of(72)
     idx = jnp.where(lane < 96, lane >> 1, (lane >> 1) + 64)
@@ -729,7 +740,7 @@
     one.sweep(y1, x1)
     one.sweep(x1, y1)
 
-    for r in range(0, 144, 48):
+    def prolonged(r):
         idx = lane_of(48) >> 1
         for c in range(2):
             v = y1[0, c, 8 + r : 56 + r, :]
@@ -737,6 +748,7 @@
                 w = take(v, idx + 64 * t)
                 up[t, c, pl.ds(8 + 2 * r, 48, 2), :] = w
                 up[t, c, pl.ds(9 + 2 * r, 48, 2), :] = w
+
     def corrected(lo, hi):
         for r, n in fine.chunks(lo, hi):
             for t in range(2):
@@ -744,6 +756,8 @@
                 for c in range(2):
                     y0[t, c, pl.ds(r, n), :] = y0[t, c, pl.ds(r, n), :] + m * up[t, c, pl.ds(r, n), :]
 
+    prolonged(0)
+    prolonged(48)
     corrected(8, 168)
     fine.sweep(y0, x0, 16, 160)
 
@@ -751,6 +765,7 @@
     before = list(sent)
     for h in range(2):
         if h == 1:
+            prolonged(96)
             corrected(168, 296)
             fine.sweep(y0, x0, 160, 288)
         for r in range(128 * h, 128 * h + 128, 32):

time: 41.4 us -> 40.3 us (0.973)
  Pallas kernels: 39.3 us -> 38.2 us
    pallas_call x1, Pallas kernels: 39.3 us -> 38.2 us  [on_device(): pl.pallas_call(kernel, out_shape=(pltpu.VMEM((2, 256, 128), f32), pltpu.V...]
where the time goes in v4:
time: 40.3 us; the launch traced here: 40.2 us
  Pallas kernels  38.2 us (95%)
  local copies, waits for them, and re-layouts  1.41 us (3%)
  between operations  0.64 us (2%)
    pallas_call x1, Pallas kernels, on_device(): pl.pallas_call(kernel, out_shape=(pltpu.VMEM((2, 256, 128), f32), pltpu.V...  38.2 us
    unnamed x2, local copies, waits for them, and re-layouts  1.41 us

profile of v4, /device:TPU:1, one launch (start us, length us, event | category | flops | bytes accessed | tf_op | source)
XLA Modules:
  0.0 40.2 jit_solution(192095946325859769)
XLA Ops:
  0.6 38.2 %shard_map.104 = (f32[2,256,128]{2,1,0:T(8,128)S(1)}, f32[2,16,2048]{2,1,0:T(8,128)S(1)}) custom-call(f32[2,256,128]{2,1,0:T(8,128)} %vel_h.1, f32[2,256,128]{2,1,0:T(8,128)} %res_h.1, f32[256,128]{1,0:T(8,128)} %east_h.1, f32[256,128]{1,0:T(8,128)} %north_h.1, f32[256,128]{1,0:T(8,128)} %cor_h.1, s32[256,128]{1,0:T(8,128)} %land_h.1, f32[2,16,2048]{2,1,0:T(8,128)} %ocv_h.1, ...), custom_call_target="tpu_custom_call" | custom-call | tf_op jit(solution)/shard_map/pallas_call | solution.py:833
  38.8 0.7 %copy.13 = f32[2,256,128]{2,1,0:T(8,128)} copy(f32[2,256,128]{2,1,0:T(8,128)S(1)} %get-tuple-element.2) | data formatting | bytes 524288
  39.5 0.7 %copy.14 = f32[2,16,2048]{2,1,0:T(8,128)} copy(f32[2,16,2048]{2,1,0:T(8,128)S(1)} %get-tuple-element.3) | data formatting | bytes 524288

commit v5 on v4

--- a/solution.py
+++ b/solution.py
@@ -800,6 +800,18 @@
         c.wait_send()
 
 
+def write_out(v, s, v_h, s_h, sem):
+    copies = [
+        pltpu.make_async_copy(src.at[c], dst.at[c], sem.at[2 * k + c])
+        for k, (src, dst) in enumerate(((v, v_h), (s, s_h)))
+        for c in range(2)
+    ]
+    for c in copies:
+        c.start()
+    for c in copies:
+        c.wait()
+
+
 def on_device(velocity, residual, east, north, coriolis, land, ocean_velocity, owner, tile_drag):
     f32 = jnp.float32
 
@@ -830,7 +842,7 @@
     scratch.append(pltpu.SemaphoreType.REGULAR((8,)))
     hbm = pl.BlockSpec(memory_space=pltpu.HBM)
     vmem = pl.BlockSpec(memory_space=pltpu.VMEM)
-    return pl.pallas_call(
+    v, s = pl.pallas_call(
         kernel,
         out_shape=(pltpu.VMEM((2, 256, 128), f32), pltpu.VMEM((2, 16, 2048), f32)),
         in_specs=[hbm] * 9,
@@ -840,6 +852,14 @@
             collective_id=0, has_side_effects=True, vmem_limit_bytes=63 * 1024 * 1024
         ),
     )(velocity, residual, east, north, coriolis, land, ocean_velocity, owner, tile_drag)
+    return pl.pallas_call(
+        write_out,
+        out_shape=(pltpu.HBM(v.shape, f32), pltpu.HBM(s.shape, f32)),
+        in_specs=[vmem, vmem],
+        out_specs=(hbm, hbm),
+        scratch_shapes=[pltpu.SemaphoreType.DMA((4,))],
+        compiler_params=pltpu.CompilerParams(vmem_limit_bytes=1024 * 1024),
+    )(v, s)
 
 
 def solution(mesh):

time: 40.3 us -> 39.8 us (0.988)
  local copies, waits for them, and re-layouts: 1.41 us -> 0 us
  Pallas kernels: 38.2 us -> 39 us
    unnamed x2 -> x0, local copies, waits for them, and re-layouts: 1.41 us -> none
    pallas_call x0 -> x1, Pallas kernels: none -> 0.82 us  [on_device(): pl.pallas_call(write_out, out_shape=(pltpu.HBM(v.shape, f32), pltpu.HBM(s...]
where the time goes in v5:
time: 39.8 us; the launch traced here: 39.6 us
  Pallas kernels  39 us (98%)
  between operations  0.64 us (2%)
    pallas_call x1, Pallas kernels, on_device(): pl.pallas_call(kernel, out_shape=(pltpu.VMEM((2, 256, 128), f32), pltpu.V...  38.2 us
    pallas_call x1, Pallas kernels, on_device(): pl.pallas_call(write_out, out_shape=(pltpu.HBM(v.shape, f32), pltpu.HBM(s...  0.82 us

profile of v5, /device:TPU:1, one launch (start us, length us, event | category | flops | bytes accessed | tf_op | source)
XLA Modules:
  0.0 39.6 jit_solution(14373928847885784478)
XLA Ops:
  0.6 38.2 %shard_map.104 = (f32[2,256,128]{2,1,0:T(8,128)S(1)}, f32[2,16,2048]{2,1,0:T(8,128)S(1)}) custom-call(f32[2,256,128]{2,1,0:T(8,128)} %vel_h.1, f32[2,256,128]{2,1,0:T(8,128)} %res_h.1, f32[256,128]{1,0:T(8,128)} %east_h.1, f32[256,128]{1,0:T(8,128)} %north_h.1, f32[256,128]{1,0:T(8,128)} %cor_h.1, s32[256,128]{1,0:T(8,128)} %land_h.1, f32[2,16,2048]{2,1,0:T(8,128)} %ocv_h.1, ...), custom_call_target="tpu_custom_call" | custom-call | tf_op jit(solution)/shard_map/pallas_call | solution.py:845
  38.8 0.8 %shard_map.105 = (f32[2,256,128]{2,1,0:T(8,128)}, f32[2,16,2048]{2,1,0:T(8,128)}) custom-call(f32[2,256,128]{2,1,0:T(8,128)S(1)} %get-tuple-element.4.v, f32[2,16,2048]{2,1,0:T(8,128)S(1)} %get-tuple-element.5.s), custom_call_target="tpu_custom_call" | custom-call | tf_op jit(solution)/shard_map/pallas_call | solution.py:855

commit v6 on v5

--- a/solution.py
+++ b/solution.py
@@ -23,7 +23,8 @@
 FIRST = [118, 118, 118, 118, 118, 117]
 TOP, OWN, BOT, END = 8, 24, 280, 296
 NEIGHBOURS = [(1, 1), (-1, 1), (1, -1), (-1, -1), (1, 0), (-1, 0), (0, 1), (0, -1)]
-FAR_FIRST = sorted(range(1, GX), key=lambda o: -min(o % 4, 4 - o % 4) - min(o // 4, 4 - o // 4))
+FAR_X = (5, -5, 2, -2, 3, -3, 1, -1, 4, -4)
+FAR_Y = (3, -3, 2, -2, 1, -1)
 
 
 def lane_of(n):
@@ -200,13 +201,13 @@
 
     def greet(step):
         for k, (dx, dy) in enumerate(((1, 0), (0, 1))):
-            if step < 4 - k:
+            if step < 3:
                 for sign in (1, -1):
                     signal(known.at[2 * step + k], sign * dx << step, sign * dy << step)
 
     def greeted(step):
         for k, (dx, dy) in enumerate(((1, 0), (0, 1))):
-            if step < 4 - k:
+            if step < 3:
                 dx, dy = dx << step, dy << step
                 pl.semaphore_wait(known.at[2 * step + k], one_if(dx, dy) + one_if(-dx, -dy))
 
@@ -291,6 +292,22 @@
                 gb2[k, c] = blank[0:32]
             for c in range(2):
                 corner[q + c] = blank[0:16]
+
+    for k, o in enumerate(FAR_X):
+
+        @pl.when(jnp.logical_not(inside(-o, 0)))
+        def _(k=k):
+            g1b[k + 1] = zero
+            g1c[k + 1, 0] = zero
+            g1c[k + 1, 1] = zero
+
+    for q in range(GY):
+
+        @pl.when(jnp.logical_or(gy > q + 3, gy < q - 3))
+        def _(q=q):
+            b5[8 * q : 8 * q + 8, :] = zero
+            for k in range(2):
+                c5[k, 8 * q : 8 * q + 8, :] = zero
 
     whole[0:8, :] = zero
     whole[72:80, :] = zero
@@ -466,8 +483,6 @@
         fine.start(r, n, fine.setup(lambda t, r, n: ocean(t, r, n) > 0.5, r, n))
     fine.sweep(x0, y0)
     fine.residual(y0, ocean)
-    greeted(2)
-    greet(3)
 
     def single(lc, lb, lw, x, y, rr, rows, shift, chunk):
         return Level(
@@ -539,9 +554,9 @@
     for k, (dx, dy) in enumerate(NEIGHBOURS):
         res_in.append(send(m2, gb2.at[1 - dy, 1 - dx], b2_s.at[k], b2_r.at[k], (dx, dy)))
 
-    greeted(3)
+    greeted(2)
     gat_c = [
-        send_all(g1c.at[0], g1c.at[o], c1_s.at[o - 1], c1_r.at[o - 1], o, 0) for o in FAR_FIRST
+        send(g1c.at[0], g1c.at[k + 1], c1_s.at[k], c1_r.at[k], (o, 0)) for k, o in enumerate(FAR_X)
     ]
     for c in coef_in:
         c.wait_recv()
@@ -591,9 +606,9 @@
             lev.setup(masks[lev], r, n)
 
     def total(g):
-        parts = [g[k] for k in range(GX)]
+        parts = [g[k] for k in range(len(FAR_X) + 1)]
         while len(parts) > 1:
-            parts = [parts[i] + parts[i + 1] for i in range(0, len(parts), 2)]
+            parts = [sum(parts[i + 1 : i + 2], parts[i]) for i in range(0, len(parts), 2)]
         return parts[0]
 
     for c in res_in:
@@ -630,7 +645,7 @@
         u.append(take((v + roll(v, -4)) * 0.25, 8 * idx5))
     g1b[0] = jnp.where(here0, u[0], jnp.where(here1, u[1], 0.0))
     gat_b = [
-        send_all(g1b.at[0], g1b.at[o], b1_s.at[o - 1], b1_r.at[o - 1], o, 0) for o in FAR_FIRST
+        send(g1b.at[0], g1b.at[k + 1], b1_s.at[k], b1_r.at[k], (o, 0)) for k, o in enumerate(FAR_X)
     ]
     for c in gat_c:
         c.wait_recv()
@@ -638,14 +653,14 @@
     s1c[...] = total(g1c)
     c5[:, mine, :] = s1c[...]
     gat_c2 = [
-        send_all(s1c, c5.at[:, mine, :], c2_s.at[o - 1], c2_r.at[o - 1], 0, o) for o in (4, 3, 5, 2, 6, 1, 7)
+        send(s1c, c5.at[:, mine, :], c2_s.at[k], c2_r.at[k], (0, o)) for k, o in enumerate(FAR_Y)
     ]
     for c in gat_b:
         c.wait_recv()
     s1b[...] = total(g1b)
     b5[mine, :] = s1b[...]
     gat_b2 = [
-        send_all(s1b, b5.at[mine, :], bb_s.at[o - 1], bb_r.at[o - 1], 0, o) for o in (4, 3, 5, 2, 6, 1, 7)
+        send(s1b, b5.at[mine, :], bb_s.at[k], bb_r.at[k], (0, o)) for k, o in enumerate(FAR_Y)
     ]
     for c in gat_c2:
         c.wait_recv()
@@ -832,14 +847,14 @@
         vm(3, 128, 128), vm(3, 64, 128), vm(3, 32, 128), vm(3, 16, 128), vm(3, 8, 128),
         vm(64, 128), vm(3, 128, 128), vm(32, 128), vm(3, 3, 32, 128),
         *level(144), *level(128), *level(64), *level(32),
-        vm(16, 2, 8, 128), vm(2, 8, 128), vm(2, 64, 128), vm(16, 8, 128), vm(8, 128), vm(64, 128),
+        vm(11, 2, 8, 128), vm(2, 8, 128), vm(2, 64, 128), vm(11, 8, 128), vm(8, 128), vm(64, 128),
         vm(2, 32, 128), vm(6, 48, 128), vm(2, 48, 128), vm(2, 48, 128), vm(80, 128),
         vm(2, 2, 304, 128), vm(2, 24, 128), vm(2, 128, 256), vm(2, 16, 2048),
         pltpu.SemaphoreType.DMA((9,)),
     ]
-    for count in (10, 8, 4, 8, 8, 15, 7, 15, 7, 14):
+    for count in (10, 8, 4, 8, 8, 10, 6, 10, 6, 14):
         scratch += [pltpu.SemaphoreType.DMA((count,))] * 2
-    scratch.append(pltpu.SemaphoreType.REGULAR((8,)))
+    scratch.append(pltpu.SemaphoreType.REGULAR((6,)))
     hbm = pl.BlockSpec(memory_space=pltpu.HBM)
     vmem = pl.BlockSpec(memory_space=pltpu.VMEM)
     v, s = pl.pallas_call(

time: 39.8 us -> 36.8 us (0.925)
  the two profiles are of different devices: /device:TPU:1 before, /device:TPU:25 now
where the time goes in v6:
time: 36.8 us; the launch traced here: 36.7 us
  Pallas kernels  36 us (98%)
  between operations  0.64 us (2%)
    pallas_call x1, Pallas kernels, on_device(): pl.pallas_call(kernel, out_shape=(pltpu.VMEM((2, 256, 128), f32), pltpu.V...  35.2 us
    pallas_call x1, Pallas kernels, on_device(): pl.pallas_call(write_out, out_shape=(pltpu.HBM(v.shape, f32), pltpu.HBM(s...  0.82 us

profile of v6, /device:TPU:25, one launch (start us, length us, event | category | flops | bytes accessed | tf_op | source)
XLA Modules:
  0.0 36.7 jit_solution(10179493931436823345)
XLA Ops:
  0.6 35.2 %shard_map.104 = (f32[2,256,128]{2,1,0:T(8,128)S(1)}, f32[2,16,2048]{2,1,0:T(8,128)S(1)}) custom-call(f32[2,256,128]{2,1,0:T(8,128)} %vel_h.1, f32[2,256,128]{2,1,0:T(8,128)} %res_h.1, f32[256,128]{1,0:T(8,128)} %east_h.1, f32[256,128]{1,0:T(8,128)} %north_h.1, f32[256,128]{1,0:T(8,128)} %cor_h.1, s32[256,128]{1,0:T(8,128)} %land_h.1, f32[2,16,2048]{2,1,0:T(8,128)} %ocv_h.1, ...), custom_call_target="tpu_custom_call" | custom-call | tf_op jit(solution)/shard_map/pallas_call | solution.py:860
  35.9 0.8 %shard_map.105 = (f32[2,256,128]{2,1,0:T(8,128)}, f32[2,16,2048]{2,1,0:T(8,128)}) custom-call(f32[2,256,128]{2,1,0:T(8,128)S(1)} %get-tuple-element.4.v, f32[2,16,2048]{2,1,0:T(8,128)S(1)} %get-tuple-element.5.s), custom_call_target="tpu_custom_call" | custom-call | tf_op jit(solution)/shard_map/pallas_call | solution.py:870

commit v7 on v6

--- a/solution.py
+++ b/solution.py
@@ -395,7 +395,7 @@
 
     lane = lane_of(64)
     p2[...] = jnp.where(
-        lane < 32, oc2[0], jnp.where(lane < 64, roll(oc2[1], 32), roll(oc2[2], 64))
+        lane < 32, oc2[0, 0:64], jnp.where(lane < 64, roll(oc2[1, 0:64], 32), roll(oc2[2, 0:64], 64))
     )
     coef_in = []
     for k, (dx, dy) in enumerate(NEIGHBOURS):
@@ -844,7 +844,7 @@
         vm(2, 2, 304, 128), vm(2, 2, 304, 128), vm(2, 304, 128), vm(2, 304, 128), vm(2, 304, 128),
         vm(2, 2, 304, 128),
         vm(256, 128), vm(128, 128), vm(128, 128), vm(128, 128), vm(128, 128), vm(4, 16, 128),
-        vm(3, 128, 128), vm(3, 64, 128), vm(3, 32, 128), vm(3, 16, 128), vm(3, 8, 128),
+        vm(3, 136, 128), vm(3, 72, 128), vm(3, 40, 128), vm(3, 24, 128), vm(3, 8, 128),
         vm(64, 128), vm(3, 128, 128), vm(32, 128), vm(3, 3, 32, 128),
         *level(144), *level(128), *level(64), *level(32),
         vm(11, 2, 8, 128), vm(2, 8, 128), vm(2, 64, 128), vm(11, 8, 128), vm(8, 128), vm(64, 128),

time: 36.8 us -> 36.8 us (level)
  no operation moved by 1% of the time
where the time goes in v7:
time: 36.8 us; the launch traced here: 36.7 us
  Pallas kernels  36 us (98%)
  between operations  0.64 us (2%)
    pallas_call x1, Pallas kernels, on_device(): pl.pallas_call(kernel, out_shape=(pltpu.VMEM((2, 256, 128), f32), pltpu.V...  35.2 us
    pallas_call x1, Pallas kernels, on_device(): pl.pallas_call(write_out, out_shape=(pltpu.HBM(v.shape, f32), pltpu.HBM(s...  0.82 us

profile of v7, /device:TPU:25, one launch (start us, length us, event | category | flops | bytes accessed | tf_op | source)
XLA Modules:
  0.0 36.7 jit_solution(12068530769009998330)
XLA Ops:
  0.6 35.2 %shard_map.104 = (f32[2,256,128]{2,1,0:T(8,128)S(1)}, f32[2,16,2048]{2,1,0:T(8,128)S(1)}) custom-call(f32[2,256,128]{2,1,0:T(8,128)} %vel_h.1, f32[2,256,128]{2,1,0:T(8,128)} %res_h.1, f32[256,128]{1,0:T(8,128)} %east_h.1, f32[256,128]{1,0:T(8,128)} %north_h.1, f32[256,128]{1,0:T(8,128)} %cor_h.1, s32[256,128]{1,0:T(8,128)} %land_h.1, f32[2,16,2048]{2,1,0:T(8,128)} %ocv_h.1, ...), custom_call_target="tpu_custom_call" | custom-call | tf_op jit(solution)/shard_map/pallas_call | solution.py:860
  35.9 0.8 %shard_map.105 = (f32[2,256,128]{2,1,0:T(8,128)}, f32[2,16,2048]{2,1,0:T(8,128)}) custom-call(f32[2,256,128]{2,1,0:T(8,128)S(1)} %get-tuple-element.4.v, f32[2,16,2048]{2,1,0:T(8,128)S(1)} %get-tuple-element.5.s), custom_call_target="tpu_custom_call" | custom-call | tf_op jit(solution)/shard_map/pallas_call | solution.py:870

commit v8 on v7

--- a/solution.py
+++ b/solution.py
@@ -397,6 +397,56 @@
     p2[...] = jnp.where(
         lane < 32, oc2[0, 0:64], jnp.where(lane < 64, roll(oc2[1, 0:64], 32), roll(oc2[2, 0:64], 64))
     )
+    g2[1, 32:96, :] = p2[...]
+
+    lane = lane_of(8)
+    place = (lane - 4 * gx) & 63
+    idx5 = jnp.where(place < 4, place, 0)
+    here0 = jnp.logical_and(place < 4, lane < 64)
+    here1 = jnp.logical_and(place < 4, lane >= 64)
+    e5, n5, f5 = (take(oc5[p], idx5) for p in range(3))
+    g1c[0, 0] = jnp.where(here0, e5, jnp.where(here1, n5, 0.0))
+    g1c[0, 1] = jnp.where(here0, f5, 0.0)
+
+    for c in late:
+        c.wait()
+    tiles = [drag_s[k] for k in range(OTILES)]
+    for j in range(0, 2048, 512):
+        ow = owner[:, j : j + 512]
+        dr = jnp.zeros((16, 512), jnp.float32)
+        for k in range(OTILES):
+            dr = jnp.where(ow == k, tiles[k], dr)
+        drag[:, j : j + 512] = dr
+
+    greeted(0)
+    greet(1)
+    greeted(1)
+    greet(2)
+
+    lane = lane_of(16)
+    col = jnp.where(lane < 64, lane + 128, lane - 128) + 128 * gx
+    beside = within(col, 0, 128 * GX)
+    near = jnp.logical_and(beside, jnp.logical_or(lane < 10, lane >= 118))
+    right = is_right(16)
+
+    def spread(packed, r, beside, near):
+        for p in range(6):
+            v = roll(packed, FIRST[p] - BASE[p])
+            if p == OC:
+                v = jnp.where(near, v, 0.0)
+            elif p in (NN, EE):
+                v = jnp.where(beside, v, 0.0)
+            p0[1, p, r : r + 16, :] = v
+
+    for k in range(4):
+        for c in side_in[k]:
+            c.wait_recv()
+        for r in range(32 * k, 32 * k + 32, 16):
+            a, b = got_l[r : r + 16, :], got_r[r : r + 16, :]
+            spread(jnp.where(right, a, b), OWN + r, beside, near)
+            spread(jnp.where(right, roll(a, -11), roll(b, 11)), OWN + 128 + r, beside, near)
+    for c in rows_in + edge_in:
+        c.wait_recv()
     coef_in = []
     for k, (dx, dy) in enumerate(NEIGHBOURS):
         if dy == 0:
@@ -406,56 +456,6 @@
         else:
             src, dst = p2.at[0:32, :], g2.at[1 - dx, 96:128, :]
         coef_in.append(send(src, dst, p2_s.at[k], p2_r.at[k], (dx, dy)))
-    g2[1, 32:96, :] = p2[...]
-
-    lane = lane_of(8)
-    place = (lane - 4 * gx) & 63
-    idx5 = jnp.where(place < 4, place, 0)
-    here0 = jnp.logical_and(place < 4, lane < 64)
-    here1 = jnp.logical_and(place < 4, lane >= 64)
-    e5, n5, f5 = (take(oc5[p], idx5) for p in range(3))
-    g1c[0, 0] = jnp.where(here0, e5, jnp.where(here1, n5, 0.0))
-    g1c[0, 1] = jnp.where(here0, f5, 0.0)
-
-    for c in late:
-        c.wait()
-    tiles = [drag_s[k] for k in range(OTILES)]
-    for j in range(0, 2048, 512):
-        ow = owner[:, j : j + 512]
-        dr = jnp.zeros((16, 512), jnp.float32)
-        for k in range(OTILES):
-            dr = jnp.where(ow == k, tiles[k], dr)
-        drag[:, j : j + 512] = dr
-
-    greeted(0)
-    greet(1)
-    greeted(1)
-    greet(2)
-
-    lane = lane_of(16)
-    col = jnp.where(lane < 64, lane + 128, lane - 128) + 128 * gx
-    beside = within(col, 0, 128 * GX)
-    near = jnp.logical_and(beside, jnp.logical_or(lane < 10, lane >= 118))
-    right = is_right(16)
-
-    def spread(packed, r, beside, near):
-        for p in range(6):
-            v = roll(packed, FIRST[p] - BASE[p])
-            if p == OC:
-                v = jnp.where(near, v, 0.0)
-            elif p in (NN, EE):
-                v = jnp.where(beside, v, 0.0)
-            p0[1, p, r : r + 16, :] = v
-
-    for k in range(4):
-        for c in side_in[k]:
-            c.wait_recv()
-        for r in range(32 * k, 32 * k + 32, 16):
-            a, b = got_l[r : r + 16, :], got_r[r : r + 16, :]
-            spread(jnp.where(right, a, b), OWN + r, beside, near)
-            spread(jnp.where(right, roll(a, -11), roll(b, 11)), OWN + 128 + r, beside, near)
-    for c in rows_in + edge_in:
-        c.wait_recv()
     for k, r, there in ((0, TOP, gy > 0), (2, BOT, gy < GY - 1)):
         keep = jnp.where(there, 1, 0)
         spread(
@@ -494,7 +494,7 @@
             lw.at[0:1], lw.at[1:2], lw.at[2:3], x, y, rr, chunk,
         )
 
-    one = single(l1c, l1b, l1w, x1, y1, rr1, 144, 1, 48)
+    one = single(l1c, l1b, l1w, x1, y1, rr1, 144, 1, 24)
     for r, n in ((0, 8), (8, 64), (72, 64), (136, 8)):
         idx = (2 * lane_of(n)) & 127
         low = lane_of(n) < 64

time: 36.8 us -> 36.5 us (level)
  the two profiles are of different devices: /device:TPU:25 before, /device:TPU:24 now
where the time goes in v8:
time: 36.5 us; the launch traced here: 36.4 us
  Pallas kernels  35.7 us (98%)
  between operations  0.64 us (2%)
    pallas_call x1, Pallas kernels, on_device(): pl.pallas_call(kernel, out_shape=(pltpu.VMEM((2, 256, 128), f32), pltpu.V...  34.9 us
    pallas_call x1, Pallas kernels, on_device(): pl.pallas_call(write_out, out_shape=(pltpu.HBM(v.shape, f32), pltpu.HBM(s...  0.82 us

profile of v8, /device:TPU:24, one launch (start us, length us, event | category | flops | bytes accessed | tf_op | source)
XLA Modules:
  0.0 36.4 jit_solution(14225792701770568462)
XLA Ops:
  0.6 34.9 %shard_map.104 = (f32[2,256,128]{2,1,0:T(8,128)S(1)}, f32[2,16,2048]{2,1,0:T(8,128)S(1)}) custom-call(f32[2,256,128]{2,1,0:T(8,128)} %vel_h.1, f32[2,256,128]{2,1,0:T(8,128)} %res_h.1, f32[256,128]{1,0:T(8,128)} %east_h.1, f32[256,128]{1,0:T(8,128)} %north_h.1, f32[256,128]{1,0:T(8,128)} %cor_h.1, s32[256,128]{1,0:T(8,128)} %land_h.1, f32[2,16,2048]{2,1,0:T(8,128)} %ocv_h.1, ...), custom_call_target="tpu_custom_call" | custom-call | tf_op jit(solution)/shard_map/pallas_call | solution.py:860
  35.5 0.8 %shard_map.105 = (f32[2,256,128]{2,1,0:T(8,128)}, f32[2,16,2048]{2,1,0:T(8,128)}) custom-call(f32[2,256,128]{2,1,0:T(8,128)S(1)} %get-tuple-element.4.v, f32[2,16,2048]{2,1,0:T(8,128)S(1)} %get-tuple-element.5.s), custom_call_target="tpu_custom_call" | custom-call | tf_op jit(solution)/shard_map/pallas_call | solution.py:870
